TPU v7x, 32 devices: a whole 2x2x4 slice. The times are simulated.
32 devices in a mesh: ctx: 16 (over z, y, core), fsdp: 2 (over x).
Axes of the slice: x: 2, y: 2, z: 4, core: 2. Of those that a mesh axis runs over, the one named last changes fastest.
Arguments:
- tokens: bfloat16 [2, 2048, 768], P('fsdp', 'ctx'), may hold values from -6 to 6
- cotangent: bfloat16 [2, 2048, 768], P('fsdp', 'ctx'), may hold values from -6 to 6
- lengths: int32 [2, 4], P('fsdp'), may hold values from 1 to 1024, 2048 in all within a row
- dealing: int32 [2, 2048], P('fsdp', 'ctx'), may hold values from 0 to 2047, each once within a row
- gain_one: bfloat16 [768], P('fsdp'), may hold values from 0.25 to 1.75
- w_query: bfloat16 [768, 768], P('fsdp'), may hold values from -0.109375 to 0.109375
- w_key: bfloat16 [768, 768], P('fsdp'), may hold values from -0.109375 to 0.109375
- w_value: bfloat16 [768, 768], P('fsdp'), may hold values from -0.21875 to 0.21875
- w_out: bfloat16 [768, 768], P('fsdp'), may hold values from -0.875 to 0.875
- gain_two: bfloat16 [768], P('fsdp'), may hold values from 0.25 to 1.75
- w_in: bfloat16 [768, 3072], P('fsdp'), may hold values from -0.21875 to 0.21875
- w_ff: bfloat16 [3072, 768], P('fsdp'), may hold values from -0.15625 to 0.15625
- rel_table: bfloat16 [32, 12], P('fsdp'), may hold values from -4 to 4
Outputs:
- output: bfloat16 [2, 2048, 768], P('fsdp', 'ctx')
- grad_tokens: float32 [2, 2048, 768], P('fsdp', 'ctx')
- grad_gain_one: float32 [768], P('fsdp')
- grad_w_query: float32 [768, 768], P('fsdp')
- grad_w_key: float32 [768, 768], P('fsdp')
- grad_w_value: float32 [768, 768], P('fsdp')
- grad_w_out: float32 [768, 768], P('fsdp')
- grad_gain_two: float32 [768], P('fsdp')
- grad_w_in: float32 [768, 3072], P('fsdp')
- grad_w_ff: float32 [3072, 768], P('fsdp')
- grad_rel_table: float32 [32, 12], P('fsdp')
Inputs may be any that keep to these rules, and one draw needn't show every extreme that they name: Each group's 4 lengths add up to 2048 and the longest is 1024. `dealing`: each group's row is a permutation of the packed places 0 to 2047.
All inputs are finite; a program needn't handle non-finite values.
Results may differ from a plain program's by a relative error of at most 0.018.
Values may be sent and summed in bfloat16 or wider, within the bound.
No kernel may reach another device: no remote copies, remote signals or barrier semaphores. Data moves between devices by JAX's collectives and lax.ppermute only.
A program may use at most 256 MiB of HBM per device.

v0:
```python
import functools
import jax
import jax.numpy as jnp
from jax import lax
from jax.experimental import pallas as pl
from jax.experimental.pallas import tpu as pltpu
from jax.sharding import PartitionSpec as P

BUCKETS = 32
PIECES = 16
EPS = 1e-06
NEG = -1000000000.0
THRESHOLDS = (1, 2, 3, 4, 5, 6, 7, 8, 12, 16, 23, 32, 46, 64, 91)
VMEM_BYTES = 50 * 1024 * 1024


def cost_of(micros):
    return pl.CostEstimate(flops=int(micros * 8e8), bytes_accessed=int(micros * 2.5e6), transcendentals=0)


def dot_nt(left, right):
    return lax.dot_general(left, right, (((1,), (1,)), ((), ())), preferred_element_type=jnp.float32)


def dot_tn(left, right):
    return lax.dot_general(left, right, (((0,), (0,)), ((), ())), preferred_element_type=jnp.float32)


def pair_rows(block, half):
    lane = lax.broadcasted_iota(jnp.int32, block.shape, 1)
    zero = jnp.zeros_like(block)
    return jnp.concatenate(
        [jnp.where(lane < half, block, zero), jnp.where(lane < half, zero, block)], axis=0
    )


def pair_blocks(acc, half, rows):
    return jnp.concatenate([acc[:half, :rows], acc[half:, rows:]], axis=0)


def bias_of(row, index):
    return jnp.take_along_axis(jnp.broadcast_to(row, index.shape), index, axis=1)


def fill_rows(out_ref, j, own, got, more, spot_ref):
    rows, part = own.shape[0], got.shape[0]
    other = (1 - spot_ref[0]) * rows
    out_ref[j, pl.ds(pl.multiple_of(spot_ref[0] * rows, 64), rows), :] = own
    out_ref[j, pl.ds(pl.multiple_of(other + spot_ref[1] * part, 64), part), :] = got
    out_ref[j, pl.ds(pl.multiple_of(other + (1 - spot_ref[1]) * part, 64), part), :] = more


def project_kernel(count, total, seqs, spot_ref, *refs):
    pieces, refs = refs[:PIECES], refs[PIECES:]
    gain_ref, wq_ref, wk_ref, wv_ref, got_ref, more_ref = refs[:6]
    made_ref, idx_ref, normed_ref, full_ref, rows_scr, place_scr, own_scr = refs[6:]
    width = gain_ref.shape[1]
    rows = normed_ref.shape[0]
    outer, inner = pl.program_id(0), pl.program_id(1)

    for group in range(PIECES // count):

        @pl.when(inner == group)
        def _():
            for j in range(count):
                held = pieces[group * count + j][0]
                rows_scr[j * rows : (j + 1) * rows, :] = held[:rows]
                place_scr[j : j + 1, :] = held[rows:].astype(jnp.float32)[:1, : 2 * rows]

    spots = place_scr[...]
    spots = spots[:, :rows] * 128.0 + spots[:, rows:]
    end = 0
    begin, segment = jnp.zeros_like(spots), jnp.zeros_like(spots)
    for j in range(seqs):
        end = end + spot_ref[2 + j]
        passed = spots >= end.astype(jnp.float32)
        begin = jnp.where(passed, end.astype(jnp.float32), begin)
        segment = jnp.where(passed, segment + 1.0, segment)
    marks = spots - begin + segment * (2.0 * total)

    @pl.when((outer == 0) & (inner == 0))
    def _():
        own_scr[...] = marks[:1, :]
        for j, ref in enumerate((wq_ref, wk_ref, wv_ref)):
            fill_rows(full_ref, j, ref[...], got_ref[j], more_ref[j], spot_ref)

    values = rows_scr[...].astype(jnp.float32)
    inverse = lax.rsqrt(jnp.mean(values * values, axis=1, keepdims=True) + EPS)
    normed = (values * inverse * gain_ref[...]).astype(jnp.bfloat16)
    shape = (count, rows, width)
    for j in range(3):
        made = jnp.dot(normed, full_ref[j], preferred_element_type=jnp.float32)
        made_ref[:, :, j * width : (j + 1) * width] = made.astype(jnp.bfloat16).reshape(shape)

    @pl.when((outer == 0) & (inner == 0))
    def _():
        normed_ref[...] = normed[:rows]

    turned = jnp.transpose(marks)
    for j in range(count):
        offset = turned[:, j : j + 1] - own_scr[...]
        distance = jnp.abs(offset)
        bucket = jnp.where(offset > 0, BUCKETS // 2, 0)
        for threshold in THRESHOLDS:
            bucket = bucket + (distance >= threshold).astype(jnp.int32)
        idx_ref[j] = jnp.where(distance >= total, BUCKETS, bucket)


def project(spot, pieces, gain, weights, got, more, rows, total, seqs, count=4):
    devices, tall, width = pieces[0].shape
    held, part = weights[0].shape[0], got.shape[1]
    fixed = lambda i, j, spot: (0, 0)
    fixed3 = lambda i, j, spot: (0, 0, 0)
    moving = lambda i, j, spot: (j, i, 0)
    return pl.pallas_call(
        functools.partial(project_kernel, count, total, seqs),
        grid_spec=pltpu.PrefetchScalarGridSpec(
            num_scalar_prefetch=1,
            grid=(devices, PIECES // count),
            in_specs=[pl.BlockSpec((1, tall, width), lambda i, j, spot: (i, 0, 0))] * PIECES
            + [
                pl.BlockSpec((1, width), fixed),
                pl.BlockSpec((held, width), fixed),
                pl.BlockSpec((held, width), fixed),
                pl.BlockSpec((held, width), fixed),
                pl.BlockSpec((3, part, width), fixed3),
                pl.BlockSpec((3, part, width), fixed3),
            ],
            out_specs=[
                pl.BlockSpec((count, rows, 3 * width), moving),
                pl.BlockSpec((count, rows, rows), moving),
                pl.BlockSpec((rows, width), fixed),
                pl.BlockSpec((3, width, width), fixed3),
            ],
            scratch_shapes=[
                pltpu.VMEM((count * rows, width), jnp.bfloat16),
                pltpu.VMEM((8, 2 * rows), jnp.float32),
                pltpu.VMEM((1, rows), jnp.float32),
            ],
        ),
        out_shape=[
            jax.ShapeDtypeStruct((PIECES, devices * rows, 3 * width), jnp.bfloat16),
            jax.ShapeDtypeStruct((PIECES, devices * rows, rows), jnp.int32),
            jax.ShapeDtypeStruct((rows, width), jnp.bfloat16),
            jax.ShapeDtypeStruct((3, width, width), jnp.bfloat16),
        ],
        compiler_params=pltpu.CompilerParams(vmem_limit_bytes=VMEM_BYTES),
        cost_estimate=cost_of(0.7 * PIECES * devices),
        name="project",
    )(spot, *pieces, gain, *weights, got, more)


def close_kernel(spot_ref, attn_ref, x_ref, gain_ref, w_ref, got_ref, more_ref, resid_ref, normed_ref, attn_b_ref, full_ref):
    fill_rows(full_ref, 0, w_ref[...], got_ref[0], more_ref[0], spot_ref)
    attn = attn_ref[...].astype(jnp.bfloat16)
    attn_b_ref[...] = attn
    resid = x_ref[...].astype(jnp.float32) + jnp.dot(
        attn, full_ref[0], preferred_element_type=jnp.float32
    )
    resid_ref[...] = resid
    inverse = lax.rsqrt(jnp.mean(resid * resid, axis=1, keepdims=True) + EPS)
    normed_ref[...] = (resid * inverse * gain_ref[...]).astype(jnp.bfloat16)


def close(spot, attn, tokens, gain, weight, got, more):
    rows, width = attn.shape
    held, part = weight.shape[0], got.shape[1]
    whole = lambda i, spot: (0, 0)
    first = lambda i, spot: (0, 0, 0)
    return pl.pallas_call(
        close_kernel,
        grid_spec=pltpu.PrefetchScalarGridSpec(
            num_scalar_prefetch=1,
            grid=(1,),
            in_specs=[
                pl.BlockSpec((rows, width), whole),
                pl.BlockSpec((rows, width), whole),
                pl.BlockSpec((1, width), whole),
                pl.BlockSpec((held, width), whole),
                pl.BlockSpec((1, part, width), first),
                pl.BlockSpec((1, part, width), first),
            ],
            out_specs=[
                pl.BlockSpec((rows, width), whole),
                pl.BlockSpec((rows, width), whole),
                pl.BlockSpec((rows, width), whole),
                pl.BlockSpec((1, width, width), first),
            ],
        ),
        out_shape=[
            jax.ShapeDtypeStruct((rows, width), jnp.float32),
            jax.ShapeDtypeStruct((rows, width), jnp.bfloat16),
            jax.ShapeDtypeStruct((rows, width), jnp.bfloat16),
            jax.ShapeDtypeStruct((1, width, width), jnp.bfloat16),
        ],
        compiler_params=pltpu.CompilerParams(vmem_limit_bytes=VMEM_BYTES),
        cost_estimate=cost_of(2),
        name="close",
    )(spot, attn, tokens, gain, weight, got, more)


def branch_kernel(part_ref, got_ref, resid_ref, cot_ref, gain_ref, out_ref, attn_ref, lse_ref, payload_ref, delta_ref, grad_ref, branch_ref, gain_grad_ref):
    f32, bf16 = jnp.float32, jnp.bfloat16
    rows, width = resid_ref.shape
    heads = lse_ref.shape[0]
    size = width // heads
    resid = resid_ref[...]
    normed_grad = part_ref[...] + got_ref[...].astype(f32)
    inverse = lax.rsqrt(jnp.mean(resid * resid, axis=1, keepdims=True) + EPS)
    gain_grad_ref[...] = jnp.sum(normed_grad * resid * inverse, axis=0, keepdims=True)
    scaled = normed_grad * gain_ref[...]
    mean = jnp.mean(scaled * resid, axis=1, keepdims=True)
    grad = cot_ref[...].astype(f32) + inverse * (scaled - resid * (inverse * inverse * mean))
    grad_ref[...] = grad
    branch = grad.astype(bf16)
    branch_ref[...] = branch
    attn_grad = dot_nt(branch, out_ref[0]).astype(bf16)
    payload_ref[:, :width] = attn_grad
    product = attn_grad.astype(f32) * attn_ref[...]
    high = product.astype(bf16)
    low = (product - high.astype(f32)).astype(bf16)

    def member(shape, at_row, at_col):
        row = lax.broadcasted_iota(jnp.int32, shape, 0)
        col = lax.broadcasted_iota(jnp.int32, shape, 1)
        return jnp.where(at_row(row) == at_col(col), 1.0, 0.0).astype(bf16)

    padded = 16
    by_head = member((padded, width), lambda r: r, lambda c: c // size)
    delta = (dot_nt(by_head, high) + dot_nt(by_head, low))[:heads]
    delta_ref[...] = delta
    col = lax.broadcasted_iota(jnp.int32, (rows, 128), 1)
    aux = jnp.zeros((rows, 128), f32)
    for first, values in ((0, lse_ref[...]), (64, delta)):
        values = jnp.concatenate([values, jnp.zeros((padded - heads, rows), f32)], axis=0)
        high = values.astype(bf16)
        low = (values - high.astype(f32)).astype(bf16)
        for odd, half in ((0, high), (1, low)):
            to_col = member((padded, 128), lambda r: first + odd + 2 * r, lambda c: c)
            aux = aux + dot_tn(half, to_col)
    payload_ref[:, width:] = aux.astype(bf16)


def branch(part, got, resid, cotangent, gain, full_out, attn, lse):
    rows, width = resid.shape
    heads = lse.shape[0]
    return pl.pallas_call(
        branch_kernel,
        grid=(1,),
        in_specs=[
            pl.BlockSpec((rows, width), lambda i: (0, 0)),
            pl.BlockSpec((rows, width), lambda i: (0, 0)),
            pl.BlockSpec((rows, width), lambda i: (0, 0)),
            pl.BlockSpec((rows, width), lambda i: (0, 0)),
            pl.BlockSpec((1, width), lambda i: (0, 0)),
            pl.BlockSpec((1, width, width), lambda i: (0, 0, 0)),
            pl.BlockSpec((rows, width), lambda i: (0, 0)),
            pl.BlockSpec((heads, rows), lambda i: (0, 0)),
        ],
        out_specs=[
            pl.BlockSpec((rows, width + 128), lambda i: (0, 0)),
            pl.BlockSpec((heads, rows), lambda i: (0, 0)),
            pl.BlockSpec((rows, width), lambda i: (0, 0)),
            pl.BlockSpec((rows, width), lambda i: (0, 0)),
            pl.BlockSpec((1, width), lambda i: (0, 0)),
        ],
        out_shape=[
            jax.ShapeDtypeStruct((rows, width + 128), jnp.bfloat16),
            jax.ShapeDtypeStruct((heads, rows), jnp.float32),
            jax.ShapeDtypeStruct((rows, width), jnp.float32),
            jax.ShapeDtypeStruct((rows, width), jnp.bfloat16),
            jax.ShapeDtypeStruct((1, width), jnp.float32),
        ],
        compiler_params=pltpu.CompilerParams(vmem_limit_bytes=VMEM_BYTES),
        cost_estimate=cost_of(3),
        name="branch",
    )(part, got, resid, cotangent, gain, full_out, attn, lse)


def unpack_kernel(tall, spot_ref, near_ref, far_ref, *out_refs):
    values = jnp.where(pl.program_id(0) == 0, near_ref[...], far_ref[...]).astype(jnp.float32)
    for j, ref in enumerate(out_refs):
        ref[...] = values[:, j * tall : (j + 1) * tall, :]


def unpack(spot, near, far, tall, outputs):
    half, high, width = near.shape
    step = min(4, half)
    steps = half // step

    def place(j, i, spot):
        return (jnp.bitwise_xor(j, spot[1]) * steps + i, 0, 0)

    return pl.pallas_call(
        functools.partial(unpack_kernel, tall),
        grid_spec=pltpu.PrefetchScalarGridSpec(
            num_scalar_prefetch=1,
            grid=(2, steps),
            in_specs=[
                pl.BlockSpec(
                    (step, high, width), lambda j, i, spot: (jnp.where(j == 0, i, steps - 1), 0, 0)
                ),
                pl.BlockSpec(
                    (step, high, width), lambda j, i, spot: (jnp.where(j == 0, 0, i), 0, 0)
                ),
            ],
            out_specs=[pl.BlockSpec((step, tall, width), place)] * outputs,
        ),
        out_shape=[jax.ShapeDtypeStruct((2 * half, tall, width), jnp.float32)] * outputs,
        compiler_params=pltpu.CompilerParams(vmem_limit_bytes=VMEM_BYTES),
        cost_estimate=cost_of(4),
        name="unpack",
    )(spot, near, far)


def spread_kernel(tall_ff, tall, spot_ref, full_ref, ff_ref, in_ref, out_ref):
    width = out_ref.shape[2]
    values = full_ref[...].astype(jnp.float32)
    ff_ref[...] = values[:, :tall_ff, :]
    parts = [values[:, tall_ff + j * tall : tall_ff + (j + 1) * tall, :] for j in range(5)]
    for j in range(2):
        in_ref[:, :, j * width : (j + 1) * width] = jnp.where(
            spot_ref[0] == 0, parts[j], parts[2 + j]
        )
        in_ref[:, :, (2 + j) * width : (3 + j) * width] = jnp.where(
            spot_ref[0] == 0, parts[2 + j], parts[j]
        )
    out_ref[...] = parts[4]


def spread(spot, full, tall_ff, tall):
    size, high, width = full.shape
    step = 2
    return pl.pallas_call(
        functools.partial(spread_kernel, tall_ff, tall),
        grid_spec=pltpu.PrefetchScalarGridSpec(
            num_scalar_prefetch=1,
            grid=(size // step,),
            in_specs=[pl.BlockSpec((step, high, width), lambda i, spot: (i, 0, 0))],
            out_specs=[
                pl.BlockSpec((step, tall_ff, width), lambda i, spot: (i, 0, 0)),
                pl.BlockSpec((step, tall, 4 * width), lambda i, spot: (i, 0, 0)),
                pl.BlockSpec((step, tall, width), lambda i, spot: (i, 0, 0)),
            ],
        ),
        out_shape=[
            jax.ShapeDtypeStruct((size, tall_ff, width), jnp.float32),
            jax.ShapeDtypeStruct((size, tall, 4 * width), jnp.float32),
            jax.ShapeDtypeStruct((size, tall, width), jnp.float32),
        ],
        compiler_params=pltpu.CompilerParams(vmem_limit_bytes=VMEM_BYTES),
        cost_estimate=cost_of(6),
        name="spread",
    )(spot, full)


def attend_kernel(tile, q_ref, k_ref, v_ref, idx_ref, tab_ref, o_ref, lse_ref, m_out, p_ref, s_scr, m_scr, l_scr, acc_scr):
    chunk, n_chunks = pl.program_id(1), pl.num_programs(1)
    rows = q_ref.shape[0]
    half = q_ref.shape[1] // 2
    keys = k_ref.shape[0]

    @pl.when(chunk == 0)
    def _():
        m_scr[...] = jnp.full_like(m_scr, -3.0e38)
        l_scr[...] = jnp.zeros_like(l_scr)
        acc_scr[...] = jnp.zeros_like(acc_scr)

    q_cat = pair_rows(q_ref[...], half)
    m_old = m_scr[...]
    m_tiles = jnp.full((8, 2 * rows), -3.0e38, jnp.float32)
    for t in range(keys // tile):
        rng = slice(t * tile, (t + 1) * tile)
        s = dot_nt(k_ref[rng, :], q_cat)
        index = idx_ref[rng, :]
        s = s + jnp.concatenate(
            [bias_of(tab_ref[0, j : j + 1, :], index) for j in range(2)], axis=1
        )
        s_scr[rng, :] = s
        m_tiles = jnp.maximum(m_tiles, jnp.max(s.reshape(tile // 8, 8, 2 * rows), axis=0))
    m_new = jnp.maximum(m_old, jnp.max(m_tiles, axis=0, keepdims=True))
    fade = jnp.exp(m_old - m_new)
    sums = jnp.zeros((8, 2 * rows), jnp.float32)
    acc = acc_scr[...] * fade
    for t in range(keys // tile):
        rng = slice(t * tile, (t + 1) * tile)
        p = jnp.exp(s_scr[rng, :] - m_new)
        sums = sums + jnp.sum(p.reshape(tile // 8, 8, 2 * rows), axis=0)
        p_low = p.astype(jnp.bfloat16)
        p_ref[0, rng, :] = p_low[:, :rows]
        p_ref[1, rng, :] = p_low[:, rows:]
        acc = acc + dot_tn(v_ref[rng, :], p_low)
    acc_scr[...] = acc
    l_new = l_scr[...] * fade + jnp.sum(sums, axis=0, keepdims=True)
    l_scr[...] = l_new
    m_scr[...] = m_new
    m_out[0, 0] = m_new

    @pl.when(chunk == n_chunks - 1)
    def _():
        lse_ref[0] = m_new + jnp.log(l_new)
        o_ref[...] = jnp.transpose(pair_blocks(acc / l_new, half, rows))


def attend(made, index, table, chunk_keys, tile=512):
    total, rows = index.shape
    width = made.shape[1] // 3
    heads = table.shape[0] * 2
    pairs = table.shape[0]
    wide = width // pairs
    n_chunks = total // chunk_keys
    return pl.pallas_call(
        functools.partial(attend_kernel, tile),
        grid=(pairs, n_chunks),
        in_specs=[
            pl.BlockSpec((rows, wide), lambda p, c: (0, p)),
            pl.BlockSpec((chunk_keys, wide), lambda p, c: (c, pairs + p)),
            pl.BlockSpec((chunk_keys, wide), lambda p, c: (c, 2 * pairs + p)),
            pl.BlockSpec((chunk_keys, rows), lambda p, c: (c, 0)),
            pl.BlockSpec((1, 2, 128), lambda p, c: (p, 0, 0)),
        ],
        out_specs=[
            pl.BlockSpec((rows, wide), lambda p, c: (0, p)),
            pl.BlockSpec((1, 1, 2 * rows), lambda p, c: (p, 0, 0)),
            pl.BlockSpec((1, 1, 1, 2 * rows), lambda p, c: (p, c, 0, 0)),
            pl.BlockSpec((2, chunk_keys, rows), lambda p, c: (p, c, 0)),
        ],
        out_shape=[
            jax.ShapeDtypeStruct((rows, width), jnp.float32),
            jax.ShapeDtypeStruct((pairs, 1, 2 * rows), jnp.float32),
            jax.ShapeDtypeStruct((pairs, n_chunks, 1, 2 * rows), jnp.float32),
            jax.ShapeDtypeStruct((heads, total, rows), jnp.bfloat16),
        ],
        scratch_shapes=[
            pltpu.VMEM((chunk_keys, 2 * rows), jnp.float32),
            pltpu.VMEM((1, 2 * rows), jnp.float32),
            pltpu.VMEM((1, 2 * rows), jnp.float32),
            pltpu.VMEM((wide, 2 * rows), jnp.float32),
        ],
        compiler_params=pltpu.CompilerParams(vmem_limit_bytes=VMEM_BYTES),
        cost_estimate=cost_of(0.008 * total),
        name="attend",
    )(made, made, made, index, table)


def query_back_kernel(tile, p_ref, v_ref, k_ref, da_ref, delta_ref, lse_ref, m_ref, ds_ref, dq_ref, acc_scr):
    chunk, n_chunks = pl.program_id(1), pl.num_programs(1)
    rows = da_ref.shape[0]
    half = da_ref.shape[1] // 2
    keys = v_ref.shape[0]

    @pl.when(chunk == 0)
    def _():
        acc_scr[...] = jnp.zeros_like(acc_scr)

    factor = jnp.exp(m_ref[0, 0] - lse_ref[0])
    delta = delta_ref[0]
    da_cat = pair_rows(da_ref[...], half)
    acc = acc_scr[...]
    for t in range(keys // tile):
        rng = slice(t * tile, (t + 1) * tile)
        dp = dot_nt(v_ref[rng, :], da_cat)
        p = jnp.concatenate([p_ref[0, rng, :], p_ref[1, rng, :]], axis=1).astype(jnp.float32)
        ds = ((p * factor) * (dp - delta)).astype(jnp.bfloat16)
        ds_ref[0, rng, :] = ds[:, :rows]
        ds_ref[1, rng, :] = ds[:, rows:]
        acc = acc + dot_tn(k_ref[rng, :], ds)
    acc_scr[...] = acc

    @pl.when(chunk == n_chunks - 1)
    def _():
        dq_ref[...] = jnp.transpose(pair_blocks(acc, half, rows)).astype(jnp.bfloat16)


def query_back(probs, made, payload, delta, lse, lows, chunk_keys, tile=512):
    heads, total, rows = probs.shape
    pairs = heads // 2
    width = made.shape[1] // 3
    wide = width // pairs
    n_chunks = total // chunk_keys
    return pl.pallas_call(
        functools.partial(query_back_kernel, tile),
        grid=(pairs, n_chunks),
        in_specs=[
            pl.BlockSpec((2, chunk_keys, rows), lambda p, c: (p, c, 0)),
            pl.BlockSpec((chunk_keys, wide), lambda p, c: (c, 2 * pairs + p)),
            pl.BlockSpec((chunk_keys, wide), lambda p, c: (c, pairs + p)),
            pl.BlockSpec((rows, wide), lambda p, c: (0, p)),
            pl.BlockSpec((1, 1, 2 * rows), lambda p, c: (p, 0, 0)),
            pl.BlockSpec((1, 1, 2 * rows), lambda p, c: (p, 0, 0)),
            pl.BlockSpec((1, 1, 1, 2 * rows), lambda p, c: (p, c, 0, 0)),
        ],
        out_specs=[
            pl.BlockSpec((2, chunk_keys, rows), lambda p, c: (p, c, 0)),
            pl.BlockSpec((rows, wide), lambda p, c: (0, p)),
        ],
        out_shape=[
            jax.ShapeDtypeStruct((heads, total, rows), jnp.bfloat16),
            jax.ShapeDtypeStruct((rows, width), jnp.bfloat16),
        ],
        scratch_shapes=[pltpu.VMEM((wide, 2 * rows), jnp.float32)],
        input_output_aliases={0: 0},
        compiler_params=pltpu.CompilerParams(vmem_limit_bytes=VMEM_BYTES),
        cost_estimate=cost_of(0.005 * total),
        name="query_back",
    )(probs, made, made, payload, delta, lse, lows)


def key_back_kernel(count, *refs):
    grads, auxes, refs = refs[:PIECES], refs[PIECES : 2 * PIECES], refs[2 * PIECES :]
    q_ref, idx_ref, k_ref, v_ref, tab_ref, dk_ref, dv_ref, dk_scr, dv_scr = refs
    pair, chunk, n_chunks = pl.program_id(0), pl.program_id(1), pl.num_programs(1)
    rows = k_ref.shape[0]
    wide = k_ref.shape[1]
    half = wide // 2

    @pl.when(chunk == 0)
    def _():
        dk_scr[...] = jnp.zeros_like(dk_scr)
        dv_scr[...] = jnp.zeros_like(dv_scr)

    lane = lax.broadcasted_iota(jnp.int32, (2 * rows, 128), 1)
    head = 2 * pair + (lax.broadcasted_iota(jnp.int32, (2 * rows, 128), 0) >= rows).astype(jnp.int32)
    first = (lane >= 2 * head) & (lane < 2 * head + 2)
    second = (lane >= 64 + 2 * head) & (lane < 64 + 2 * head + 2)
    take_lse = jnp.where(first, -1.0, 0.0).astype(jnp.bfloat16)
    take_delta = jnp.where(second, -1.0, 0.0).astype(jnp.bfloat16)
    k_cat = jnp.concatenate([pair_rows(k_ref[...], half), take_lse], axis=1)
    v_cat = jnp.concatenate([pair_rows(v_ref[...], half), take_delta], axis=1)
    dk, dv = dk_scr[...], dv_scr[...]
    for t in range(0, PIECES, count):
        da = jnp.concatenate([ref[...] for ref in grads[t : t + count]], axis=0)
        aux = jnp.concatenate([ref[...] for ref in auxes[t : t + count]], axis=0)
        q = q_ref[t : t + count].reshape(count * rows, wide)
        index = idx_ref[t : t + count].reshape(count * rows, rows)
        s = dot_nt(jnp.concatenate([q, aux], axis=1), k_cat)
        bias = jnp.concatenate(
            [bias_of(tab_ref[0, j : j + 1, :], index) for j in range(2)], axis=1
        )
        p = jnp.exp(s + bias)
        ds = p * dot_nt(jnp.concatenate([da, aux], axis=1), v_cat)
        dv = dv + dot_tn(da, p.astype(jnp.bfloat16))
        dk = dk + dot_tn(q, ds.astype(jnp.bfloat16))
    dk_scr[...] = dk
    dv_scr[...] = dv

    @pl.when(chunk == n_chunks - 1)
    def _():
        dk_ref[...] = jnp.transpose(pair_blocks(dk, half, rows)).astype(jnp.bfloat16)
        dv_ref[...] = jnp.transpose(pair_blocks(dv, half, rows)).astype(jnp.bfloat16)


def key_back(pieces, made, index, table, count=4):
    rows = index.shape[2]
    side, width = made.shape[1], made.shape[2] // 3
    pairs = table.shape[0]
    wide = width // pairs
    n_chunks = side // rows
    return pl.pallas_call(
        functools.partial(key_back_kernel, count),
        grid=(pairs, n_chunks),
        in_specs=[pl.BlockSpec((rows, wide), lambda p, c: (c, p))] * PIECES
        + [pl.BlockSpec((rows, 128), lambda p, c: (c, pairs))] * PIECES
        + [
            pl.BlockSpec((PIECES, rows, wide), lambda p, c: (0, c, p)),
            pl.BlockSpec((PIECES, rows, rows), lambda p, c: (0, c, 0)),
            pl.BlockSpec((rows, wide), lambda p, c: (0, pairs + p)),
            pl.BlockSpec((rows, wide), lambda p, c: (0, 2 * pairs + p)),
            pl.BlockSpec((1, 2, 128), lambda p, c: (p, 0, 0)),
        ],
        out_specs=[
            pl.BlockSpec((rows, wide), lambda p, c: (0, p)),
            pl.BlockSpec((rows, wide), lambda p, c: (0, p)),
        ],
        out_shape=[
            jax.ShapeDtypeStruct((rows, width), jnp.bfloat16),
            jax.ShapeDtypeStruct((rows, width), jnp.bfloat16),
        ],
        scratch_shapes=[
            pltpu.VMEM((wide, 2 * rows), jnp.float32),
            pltpu.VMEM((wide, 2 * rows), jnp.float32),
        ],
        compiler_params=pltpu.CompilerParams(vmem_limit_bytes=VMEM_BYTES),
        cost_estimate=cost_of(15 * n_chunks),
        name="key_back",
    )(*pieces, *pieces, made, index, made[0], made[0], table)


def norm_back(values, inverse, scale_gain, grad_normed):
    grad_gain = jnp.sum(grad_normed * values * inverse, axis=0)
    scaled = grad_normed * scale_gain
    grad_values = inverse * (
        scaled - values * inverse * inverse * jnp.mean(scaled * values, axis=1, keepdims=True)
    )
    return (grad_gain, grad_values)


def smooth_gate(values):
    return jax.nn.gelu(values, approximate=True)


def dot_f32(left, right):
    return jnp.dot(left, right, preferred_element_type=jnp.float32)


def swap_ctx(values, distance):
    size = lax.axis_size("ctx")
    return lax.ppermute(values, "ctx", [(i, i ^ distance) for i in range(size)])


def swap_pair(values):
    return lax.ppermute(values, "fsdp", [(0, 1), (1, 0)])


def in_order(where, mine, other, axis=0):
    return jnp.where(
        where == 0,
        jnp.concatenate([mine, other], axis=axis),
        jnp.concatenate([other, mine], axis=axis),
    )


def part_of(values, index, parts, axis):
    size = values.shape[axis] // parts
    return lax.dynamic_slice_in_dim(values, index * size, size, axis)


def tied(*members):
    return lax.optimization_barrier(members)


def gather_group(block, ties=(None, None, None, None)):
    size = lax.axis_size("ctx")
    quarter = size // 4
    ties = list(ties)
    block = block[None]
    distance = 2 * 2
    while distance < quarter:
        block = jnp.concatenate([block, swap_ctx(block, distance)], axis=0)
        distance *= 2
    far = [swap_ctx(block, quarter * j) for j in (1, 2, 3)]
    near = [block, swap_ctx(block, 2)]
    for j in range(3):
        if ties[j] is not None:
            far[j], ties[j] = tied(far[j], ties[j])
        near += [far[j], swap_ctx(far[j], 2)]
    if ties[3] is not None:
        near[-1], ties[3] = tied(near[-1], ties[3])
    return near + [swap_ctx(piece, 1) for piece in near], ties


def scatter_sum(blocks, tie):
    here, size = lax.axis_index("ctx"), lax.axis_size("ctx")
    low, f32 = blocks.dtype, jnp.float32
    distance = 1
    while distance < size // 4:
        mine = (here // distance) % 2
        got = swap_ctx(part_of(blocks, 1 - mine, 2, 0), distance)
        blocks = (part_of(blocks, mine, 2, 0).astype(f32) + got.astype(f32)).astype(low)
        if distance == 1:
            blocks, tie = tied(blocks, tie)
        distance *= 2
    mine = here // distance
    got = [swap_ctx(part_of(blocks, mine ^ j, 4, 0), distance * j) for j in (1, 2, 3)]
    added = part_of(blocks, mine, 4, 0).astype(f32) + sum(member.astype(f32) for member in got)
    return added.astype(low), tie


def gather_back(block):
    here, size = lax.axis_index("ctx"), lax.axis_size("ctx")
    distance = size // 4
    got = [swap_ctx(block, distance * j) for j in (1, 2, 3)]
    low_bit, high_bit = (here // distance) % 2, here // (2 * distance)
    blocks = in_order(high_bit, in_order(low_bit, block, got[0]), in_order(low_bit, got[1], got[2]))
    while distance > 2:
        distance //= 2
        blocks = in_order((here // distance) % 2, blocks, swap_ctx(blocks, distance))
    return blocks, swap_ctx(blocks, 1)


def sent_weights(*members):
    core = lax.axis_index("ctx") % 2
    return swap_pair(jnp.stack([part_of(member, core, 2, 0) for member in members]))


def shards(
    tokens,
    cotangent,
    lengths,
    dealing,
    gain_one,
    w_query,
    w_key,
    w_value,
    w_out,
    gain_two,
    w_in,
    w_ff,
    rel_table,
):
    bf16, f32 = jnp.bfloat16, jnp.float32
    size = lax.axis_size("ctx")
    pair = lax.axis_index("fsdp")
    rows, width = tokens.shape[1], tokens.shape[2]
    heads = rel_table.shape[1]
    head_size = width // heads
    pairs = heads // 2
    total = size * rows
    half_ff = w_ff.shape[0]
    half_width = w_query.shape[0]
    chunk_keys = min(total, 2048)

    spot = jnp.concatenate(
        [jnp.stack([pair, lax.axis_index("ctx") % 2]).astype(jnp.int32), lengths[0]]
    )

    dealt = dealing[0]
    place_row = jnp.concatenate([dealt // 128, dealt % 128]).astype(bf16)
    place_rows = jnp.pad(place_row[None], ((0, 7), (0, width - 2 * rows)))
    pieces = gather_group(jnp.concatenate([tokens[0], place_rows], axis=0))[0]

    small = jnp.concatenate([gain_one, gain_two, rel_table.reshape(-1)])
    small = jnp.pad(small, (0, 1024 - small.shape[0])).reshape(8, 128)
    small_other = swap_pair(small)
    small_full = jnp.stack([small.reshape(-1), small_other.reshape(-1)])
    small_full = jnp.where(pair == 0, small_full, small_full[::-1])
    gain32_one = small_full[:, :half_width].reshape(width).astype(f32)
    gain32_two = small_full[:, half_width : 2 * half_width].reshape(width).astype(f32)
    full_table = small_full[:, 2 * half_width : 2 * half_width + rel_table.size]
    full_table = full_table.reshape(2 * rel_table.shape[0], heads).astype(f32)
    got_one = sent_weights(w_query, w_key, w_value)
    more_one = swap_ctx(got_one, 1)
    pieces[4], w_out, w_in, cotangent = tied(pieces[4], w_out, w_in, cotangent)
    mine_in, other_in = (part_of(w_in, index, 2, 1) for index in (pair, 1 - pair))
    got_two = sent_weights(w_out, other_in[:, :width], other_in[:, width:])
    grad_out = cotangent[0]
    grad_out_pair = jnp.concatenate([grad_out, swap_pair(grad_out)], axis=0)

    table_t = jnp.transpose(full_table)
    back_t = jnp.concatenate(
        [table_t[:, :1], table_t[:, 17:], table_t[:, :1], table_t[:, 1:16]], axis=1
    )
    tables = [
        jnp.pad(tab, ((0, 0), (0, 128 - BUCKETS)), constant_values=NEG).reshape(pairs, 2, 128)
        for tab in (table_t, back_t)
    ]
    made, index, normed_one, w_qkv = project(
        spot,
        pieces,
        gain32_one[None],
        (w_query, w_key, w_value),
        got_one,
        more_one,
        rows,
        total,
        lengths.shape[1],
    )
    made, got_two = tied(made, got_two)
    more_two = swap_ctx(got_two, 1)
    flat_made, flat_index = made.reshape(total, 3 * width), index.reshape(total, rows)
    attn_f32, lse, lows, probs = attend(flat_made, flat_index, tables[0], chunk_keys)

    resid, normed_two, attn_b, full_out = close(
        spot, attn_f32, tokens[0], gain32_two[None], w_out, got_two, more_two
    )
    normed_pair = jnp.concatenate([normed_two, swap_pair(normed_two)], axis=0)
    core = lax.axis_index("ctx") % 2
    half_in = jnp.concatenate(
        [
            in_order(
                pair,
                mine_in[:, j * width : (j + 1) * width],
                in_order(core, got_two[1 + j], more_two[1 + j]),
            )
            for j in range(2)
        ],
        axis=1,
    )
    gate_pre = dot_f32(normed_pair, half_in)
    gate_val, gate_pull = jax.vjp(smooth_gate, gate_pre)
    active = gate_val.astype(bf16)
    grad_active = jnp.einsum("td,fd->tf", grad_out_pair, w_ff, preferred_element_type=f32)
    grad_pre = gate_pull(grad_active)[0].astype(bf16)
    grad_normed_part = jnp.einsum("tf,df->td", grad_pre, half_in, preferred_element_type=f32)
    payload, delta, grad_resid, grad_branch, grad_gain_two = branch(
        grad_normed_part[:rows],
        swap_pair(grad_normed_part[rows:].astype(bf16)),
        resid,
        grad_out,
        gain32_two[None],
        full_out,
        attn_f32,
        lse.reshape(heads, rows),
    )
    payload, active, normed_pair, grad_pre, attn_b = tied(
        payload, active, normed_pair, grad_pre, attn_b
    )

    def halves(values):
        other = swap_pair(part_of(values, 1 - pair, 2, 1))
        return jnp.concatenate([part_of(values, pair, 2, 1), other], axis=0)

    def both(values):
        return jnp.concatenate([values, swap_pair(values)], axis=0)

    def by_rows(left, right):
        return jnp.einsum("td,te->de", left, right, preferred_element_type=f32).astype(bf16)

    def blocks_of(values):
        return [
            values[:, j : j + width].reshape(size, values.shape[0] // size, width)
            for j in range(0, values.shape[1], width)
        ]

    tall = half_width // size
    tall_ff = half_ff // size
    grad_ff_part = by_rows(active, grad_out_pair)
    grad_in_part = by_rows(normed_pair, grad_pre)
    branch_other = swap_pair(
        jnp.concatenate([part_of(attn_b, 1 - pair, 2, 1), grad_branch], axis=1)
    )
    attn_pair = jnp.concatenate([part_of(attn_b, pair, 2, 1), branch_other[:, :half_width]], axis=0)
    branch_pair = jnp.concatenate([grad_branch, branch_other[:, half_width:]], axis=0)
    grad_out_part = by_rows(attn_pair, branch_pair)
    in_blocks = blocks_of(part_of(grad_in_part, pair, 2, 0)) + blocks_of(
        part_of(grad_in_part, 1 - pair, 2, 0)
    )
    ff_blocks = jnp.concatenate(
        blocks_of(grad_ff_part) + in_blocks + blocks_of(grad_out_part), axis=1
    )
    ff_tall = ff_blocks.shape[1]

    grad_scores, grad_q = query_back(
        probs, flat_made, payload, delta.reshape(pairs, 1, 2 * rows), lse, lows, chunk_keys
    )
    one_hot = (flat_index[:, :, None] == jnp.arange(BUCKETS, dtype=jnp.int32)).astype(bf16)
    grad_tab = jnp.einsum("hkq,kqb->hb", grad_scores, one_hot, preferred_element_type=f32)
    grad_pieces, ties = gather_group(
        payload, ((grad_ff_part, grad_in_part), ff_blocks, grad_q, grad_tab)
    )
    ff_blocks, grad_q, grad_tab = ties[1:]
    ff_sum = lax.psum_scatter(
        ff_blocks.reshape(size * ff_tall, width), "ctx", scatter_dimension=0, tiled=True
    )
    grad_k, grad_v = key_back(
        [piece.reshape(-1, width + 128) for piece in grad_pieces], made, index, tables[1]
    )
    out_part = dot_f32(active, w_ff)
    output = resid + out_part[:rows] + swap_pair(out_part[rows:].astype(bf16)).astype(f32)

    grads_kv = jnp.concatenate([grad_k, grad_v], axis=1)
    normed_halves = halves(normed_one)
    grad_q_part = by_rows(normed_halves, both(grad_q))
    grad_kv_part = by_rows(normed_halves, both(grads_kv))
    inputs = tokens[0].astype(f32)
    inv_one = lax.rsqrt(jnp.mean(inputs * inputs, axis=1, keepdims=True) + EPS)
    grad_normed_one = sum(
        jnp.einsum("te,de->td", member, w_qkv[j], preferred_element_type=f32)
        for j, member in enumerate((grad_q, grad_k, grad_v))
    )
    grad_gain_one, grad_input_norm = norm_back(inputs, inv_one, gain32_one, grad_normed_one)
    grad_tokens = grad_resid + grad_input_norm

    small_grads = jnp.concatenate(
        [
            grad_gain_one.reshape(2, half_width),
            grad_gain_two.reshape(2, half_width),
            jnp.transpose(grad_tab).reshape(2, rel_table.size),
        ],
        axis=1,
    )
    n_small = small_grads.shape[1]
    each = -(-n_small // size)
    small_grads = jnp.pad(small_grads, ((0, 0), (0, size * each - n_small)))
    small_pair = part_of(small_grads, pair, 2, 0) + swap_pair(part_of(small_grads, 1 - pair, 2, 0))
    small_blocks = jnp.pad(
        small_pair.astype(bf16).reshape(size, 1, each), ((0, 0), (0, 7), (0, width - each))
    )
    qkv_sum, ff_sum = scatter_sum(
        jnp.concatenate(
            blocks_of(grad_q_part) + blocks_of(grad_kv_part) + [small_blocks], axis=1
        ),
        ff_sum,
    )
    first_in, last_in = tall_ff, tall_ff + 4 * tall
    moved = swap_pair(ff_sum[tall_ff + 2 * tall : last_in])
    ff_sum = jnp.concatenate([ff_sum[: tall_ff + 2 * tall], moved, ff_sum[last_in:]], axis=0)
    ff_full = lax.all_gather(ff_sum, "ctx", axis=0, tiled=True).reshape(size, ff_tall, width)
    near_sum, far_sum = gather_back(qkv_sum)
    small_halves = [member[:, 3 * tall, :each].reshape(-1) for member in (near_sum, far_sum)]
    small_mine = in_order(spot[1], *small_halves).astype(f32)
    grad_qkv = [
        member.reshape(half_width, width) for member in unpack(spot, near_sum, far_sum, tall, 3)
    ]
    grad_ff, grad_in, grad_out_w = spread(spot, ff_full, tall_ff, tall)
    return (
        output.astype(bf16)[None],
        grad_tokens[None],
        small_mine[:half_width],
        *grad_qkv,
        grad_out_w.reshape(half_width, width),
        small_mine[half_width : 2 * half_width],
        grad_in.reshape(half_width, 4 * width),
        grad_ff.reshape(half_ff, width),
        small_mine[2 * half_width : n_small].reshape(rel_table.shape),
    )


def solution(mesh):
    spread = P("fsdp", "ctx", None)
    rows_of = P("fsdp", None)
    return jax.shard_map(
        shards,
        mesh=mesh,
        in_specs=(
            spread,
            spread,
            rows_of,
            P("fsdp", "ctx"),
            P("fsdp"),
            rows_of,
            rows_of,
            rows_of,
            rows_of,
            P("fsdp"),
            rows_of,
            rows_of,
            rows_of,
        ),
        out_specs=(
            spread,
            spread,
            P("fsdp"),
            rows_of,
            rows_of,
            rows_of,
            rows_of,
            P("fsdp"),
            rows_of,
            rows_of,
            rows_of,
        ),
        check_vma=False,
    )
```

profile of v0, /device:TPU:11, one launch (start us, length us, event | category | flops | bytes accessed | tf_op | source)
XLA Modules:
  0.0 327.8 jit_solution(17665238670850787203)
XLA Ops:
  16.7 15.7 %collective-permute-done.15 = bf16[8,128]{1,0:T(8,128)(2,1)S(1)} collective-permute-done((bf16[8,128]{1,0:T(8,128)(2,1)S(1)}, bf16[8,128]{1,0:T(8,128)(2,1)S(1)}, u32[]{:S(2)}, u32[]{:S(2)}) %collective-permute-start.15) | collective-permute-done | bytes 2080 | tf_op jit(solution)/shard_map/ppermute | solution.py:612
  37.6 2.4 collective-permute-start.11
  52.3 3.3 collective-permute-done.2.refs_3_
  58.2 16.7 %project.1 = (bf16[16,128,2304]{2,1,0:T(8,128)(2,1)}, s32[16,128,128]{2,1,0:T(8,128)}, bf16[128,768]{1,0:T(8,128)(2,1)S(1)}, bf16[3,768,768]{2,1,0:T(8,128)(2,1)}) custom-call(s32[6]{0:T(128)S(1)} %pad_add_fusion.spot_ref, bf16[1,136,768]{2,1,0:T(8,128)(2,1)S(1)} %maximum_bitcast_fusion.refs_0_, bf16[1,136,768]{2,1,0:T(8,128)(2,1)} %collective-permute-done.refs_1_, ...), custom_call_target="tpu_custom_call" | custom-call | flops 8960000000 | bytes 28000000 | tf_op jit(solution)/shard_map/project/pallas_call | solution.py:115
  75.0 2.8 collective-permute-done.18.got_ref
  80.3 17.2 %attend.1 = (f32[128,768]{1,0:T(8,128)S(1)}, f32[6,1,256]{2,1,0:T(1,128)S(1)}, f32[6,1,1,256]{3,2,1,0:T(1,128)S(1)}, bf16[12,2048,128]{2,1,0:T(8,128)(2,1)}) custom-call(bf16[2048,2304]{1,0:T(8,128)(2,1)} %bitcast.139, bf16[2048,2304]{1,0:T(8,128)(2,1)} %bitcast.140, bf16[2048,2304]{1,0:T(8,128)(2,1)} %bitcast.141, s32[2048,128]{1,0:T(8,128)S(1)} %bitcast.125, ...), custom_call_target="tpu_custom_call" | custom-call | flops 13107200000 | bytes 40960000 | tf_op jit(solution)/shard_map/attend/pallas_call | solution.py:412
  101.3 5.2 %collective-permute-done.21 = bf16[128,768]{1,0:T(8,128)(2,1)S(1)} collective-permute-done((bf16[128,768]{1,0:T(8,128)(2,1)S(1)}, bf16[128,768]{1,0:T(8,128)(2,1)S(1)}, u32[]{:S(2)}, u32[]{:S(2)}) %collective-permute-start.21) | collective-permute-done | bytes 196640 | tf_op jit(solution)/shard_map/ppermute | solution.py:612
  114.0 3.6 %collective-permute-done.22.got_ref = bf16[128,768]{1,0:T(8,128)(2,1)} collective-permute-done((bf16[128,768]{1,0:T(8,128)(2,1)}, bf16[128,768]{1,0:T(8,128)(2,1)}, u32[]{:S(2)}, u32[]{:S(2)}) %collective-permute-start.22) | collective-permute-done | bytes 196640 | tf_op jit(solution)/shard_map/ppermute | solution.py:612
  120.6 2.8 branch.1
  123.4 2.3 collective-permute-start.28
  136.1 3.1 collective-permute-start.26
  140.8 10.7 %query_back.1 = (bf16[12,2048,128]{2,1,0:T(8,128)(2,1)}, bf16[128,768]{1,0:T(8,128)(2,1)S(1)}) custom-call(bf16[12,2048,128]{2,1,0:T(8,128)(2,1)} %get-tuple-element.76.p_ref, bf16[2048,2304]{1,0:T(8,128)(2,1)} %bitcast.142, bf16[2048,2304]{1,0:T(8,128)(2,1)} %bitcast.143, ...), custom_call_target="tpu_custom_call", output_to_operand_aliasing={{0}: (0, {})} | custom-call | flops 8192000000 | bytes 25600000 | tf_op jit(solution)/shard_map/query_back/pallas_call | solution.py:481
  152.1 2.0 slice_bitcast_fusion.refs_34_.refs_35_
  154.7 2.2 collective-permute-start.32
  160.0 10.2 %fusion.21 = f32[12,32]{1,0:T(8,128)S(1)} fusion(s32[2048,128]{1,0:T(8,128)} %bitcast.124, bf16[12,2048,128]{2,1,0:T(8,128)(2,1)} %get-tuple-element.89), kind=kOutput, calls=%fused_computation.37 | convolution fusion | flops 209715200 | bytes 7341568 | tf_op jit(solution)/shard_map/hkq,kqb->hb/dot_general | solution.py:837
  172.4 2.6 fusion.16
  177.7 15.8 %key_back.1 = (bf16[128,768]{1,0:T(8,128)(2,1)S(1)}, bf16[128,768]{1,0:T(8,128)(2,1)S(1)}) custom-call(bf16[128,896]{1,0:T(8,128)(2,1)} %get-tuple-element.75.da_ref.refs_0_.refs_16_, bf16[128,896]{1,0:T(8,128)(2,1)} %bitcast.23.refs_1_.refs_17_, bf16[128,896]{1,0:T(8,128)(2,1)} %bitcast.24.refs_2_.refs_18_, bf16[128,896]{1,0:T(8,128)(2,1)} %bitcast.25.refs_3_.refs_19_, ...), custom_call_target="tpu_custom_call" | custom-call | flops 12000000000 | bytes 37500000 | tf_op jit(solution)/shard_map/key_back/pallas_call | solution.py:559
  200.8 6.9 %collective-permute-done.43 = f32[1,960]{1,0:T(1,128)S(1)} collective-permute-done((f32[1,960]{1,0:T(1,128)S(1)}, f32[1,960]{1,0:T(1,128)S(1)}, u32[]{:S(2)}, u32[]{:S(2)}) %collective-permute-start.43) | collective-permute-done | bytes 3872 | tf_op jit(solution)/shard_map/ppermute | solution.py:612
  213.9 2.3 collective-permute-done.44
  224.9 9.5 %collective-permute-done.45 = bf16[4,80,768]{2,1,0:T(8,128)(2,1)} collective-permute-done((bf16[4,80,768]{2,1,0:T(8,128)(2,1)}, bf16[4,80,768]{2,1,0:T(8,128)(2,1)}, u32[]{:S(2)}, u32[]{:S(2)}) %collective-permute-start.45) | collective-permute-done | bytes 491552 | tf_op jit(solution)/shard_map/ppermute | solution.py:608
  238.9 2.0 collective-permute-start.48
  241.6 2.7 collective-permute-done.46
  244.3 5.5 %collective-permute-done.48 = bf16[1,80,768]{2,1,0:T(8,128)(2,1)} collective-permute-done((bf16[1,80,768]{2,1,0:T(8,128)(2,1)}, bf16[1,80,768]{2,1,0:T(8,128)(2,1)}, u32[]{:S(2)}, u32[]{:S(2)}) %collective-permute-start.48) | collective-permute-done | bytes 122912 | tf_op jit(solution)/shard_map/ppermute | solution.py:608
  249.9 5.8 %collective-permute-done.47 = bf16[1,80,768]{2,1,0:T(8,128)(2,1)} collective-permute-done((bf16[1,80,768]{2,1,0:T(8,128)(2,1)S(1)}, bf16[1,80,768]{2,1,0:T(8,128)(2,1)}, u32[]{:S(2)}, u32[]{:S(2)}) %collective-permute-start.47) | collective-permute-done | bytes 122912 | tf_op jit(solution)/shard_map/ppermute | solution.py:608
  256.8 2.1 collective-permute-start.49
  260.4 9.5 %collective-permute-done.49 = bf16[1,80,768]{2,1,0:T(8,128)(2,1)} collective-permute-done((bf16[1,80,768]{2,1,0:T(8,128)(2,1)S(1)}, bf16[1,80,768]{2,1,0:T(8,128)(2,1)}, u32[]{:S(2)}, u32[]{:S(2)}) %collective-permute-start.49) | collective-permute-done | bytes 122912 | tf_op jit(solution)/shard_map/ppermute | solution.py:608
  271.2 13.3 %collective-permute-done.51 = bf16[1,80,768]{2,1,0:T(8,128)(2,1)} collective-permute-done((bf16[1,80,768]{2,1,0:T(8,128)(2,1)S(1)}, bf16[1,80,768]{2,1,0:T(8,128)(2,1)}, u32[]{:S(2)}, u32[]{:S(2)}) %collective-permute-start.51) | collective-permute-done | bytes 122912 | tf_op jit(solution)/shard_map/ppermute | solution.py:608
  286.4 2.1 collective-permute-start.52
  289.7 7.0 %collective-permute-done.52 = bf16[4,80,768]{2,1,0:T(8,128)(2,1)} collective-permute-done((bf16[4,80,768]{2,1,0:T(8,128)(2,1)}, bf16[4,80,768]{2,1,0:T(8,128)(2,1)}, u32[]{:S(2)}, u32[]{:S(2)}) %collective-permute-start.52) | collective-permute-done | bytes 491552 | tf_op jit(solution)/shard_map/ppermute | solution.py:608
  298.4 4.4 %collective-permute-start.53 = (bf16[8,80,768]{2,1,0:T(8,128)(2,1)S(1)}, bf16[8,80,768]{2,1,0:T(8,128)(2,1)}, u32[]{:S(2)}, u32[]{:S(2)}) collective-permute-start(bf16[8,80,768]{2,1,0:T(8,128)(2,1)S(1)} %maximum_select_fusion.2.near_ref), channel_id=1, source_target_pairs={{0,2},{2,0},{4,6},{6,4},{8,10},{10,8},{12,14},{14,12},{16,18},{18,... | collective-permute-start | bytes 2949128 | tf_op jit(solution)/shard_map/ppermute | solution.py:608
  307.6 4.7 %unpack.1 = (f32[16,24,768]{2,1,0:T(8,128)}, f32[16,24,768]{2,1,0:T(8,128)}, f32[16,24,768]{2,1,0:T(8,128)}) custom-call(s32[6]{0:T(128)S(1)} %copy-done.16, bf16[8,80,768]{2,1,0:T(8,128)(2,1)S(1)} %maximum_select_fusion.2.near_ref, bf16[8,80,768]{2,1,0:T(8,128)(2,1)} %collective-permute-done.53.far_ref), custom_call_target="tpu_custom_call" | custom-call | flops 3200000000 | bytes 10000000 | tf_op jit(solution)/shard_map/unpack/pallas_call | solution.py:294
  312.4 8.6 %spread.1 = (f32[16,96,768]{2,1,0:T(8,128)}, f32[16,24,3072]{2,1,0:T(8,128)}, f32[16,24,768]{2,1,0:T(8,128)}) custom-call(s32[6]{0:T(128)S(1)} %copy-done.16, bf16[16,216,768]{2,1,0:T(8,128)(2,1)} %bitcast.149), custom_call_target="tpu_custom_call" | custom-call | flops 4800000000 | bytes 15000000 | tf_op jit(solution)/shard_map/spread/pallas_call | solution.py:334
  (311 shorter events, 107.8 us)
Async XLA Ops:
  7.2 210.7 %reduce-scatter.2.cloned.1.call-start = ((), (), s32[]{:S(2)}) async-start(), calls=%async_computation.1 | async-start | bytes 5640192 | tf_op jit(solution)/shard_map/reduce_scatter | solution.py:842
  11.5 21.3 %collective-permute-start.16 = (bf16[3,192,768]{2,1,0:T(8,128)(2,1)}, bf16[3,192,768]{2,1,0:T(8,128)(2,1)}, u32[]{:S(2)}, u32[]{:S(2)}) collective-permute-start(bf16[3,192,768]{2,1,0:T(8,128)(2,1)} %pad_maximum_fusion.3), channel_id=1, source_target_pairs={{0,1},{1,0},{2,3},{3,2},{4,5},{5,4},{6,7},{7,6},{8,9},{9,8},{10,11... | collective-permute-start | bytes 2654216 | tf_op jit(solution)/shard_map/ppermute | solution.py:612
  11.8 23.5 %collective-permute-start.7 = (bf16[1,136,768]{2,1,0:T(8,128)(2,1)S(1)}, bf16[1,136,768]{2,1,0:T(8,128)(2,1)}, u32[]{:S(2)}, u32[]{:S(2)}) collective-permute-start(bf16[1,136,768]{2,1,0:T(8,128)(2,1)S(1)} %maximum_bitcast_fusion.refs_0_), channel_id=1, source_target_pairs={{0,2},{2,0},{4,6},{6,4},{8,10},{10,8},{12,14},{14,12},{16,18},{18,... | collective-permute-start | bytes 626696 | tf_op jit(solution)/shard_map/ppermute | solution.py:608
  12.9 23.7 %collective-permute-start.5 = (bf16[1,136,768]{2,1,0:T(8,128)(2,1)S(1)}, bf16[1,136,768]{2,1,0:T(8,128)(2,1)}, u32[]{:S(2)}, u32[]{:S(2)}) collective-permute-start(bf16[1,136,768]{2,1,0:T(8,128)(2,1)S(1)} %maximum_bitcast_fusion.refs_0_), channel_id=1, source_target_pairs={{0,24},{2,26},{4,28},{6,30},{8,16},{10,18},{12,20},{14,22},{16,8},... | collective-permute-start | bytes 626696 | tf_op jit(solution)/shard_map/ppermute | solution.py:608
  14.2 22.7 %collective-permute-start.3 = (bf16[1,136,768]{2,1,0:T(8,128)(2,1)S(1)}, bf16[1,136,768]{2,1,0:T(8,128)(2,1)}, u32[]{:S(2)}, u32[]{:S(2)}) collective-permute-start(bf16[1,136,768]{2,1,0:T(8,128)(2,1)S(1)} %maximum_bitcast_fusion.refs_0_), channel_id=1, source_target_pairs={{0,16},{2,18},{4,20},{6,22},{8,24},{10,26},{12,28},{14,30},{16,0},... | collective-permute-start | bytes 626696 | tf_op jit(solution)/shard_map/ppermute | solution.py:608
  15.3 17.1 %collective-permute-start.15 = (bf16[8,128]{1,0:T(8,128)(2,1)S(1)}, bf16[8,128]{1,0:T(8,128)(2,1)S(1)}, u32[]{:S(2)}, u32[]{:S(2)}) collective-permute-start(bf16[8,128]{1,0:T(8,128)(2,1)S(1)} %fusion.92), channel_id=1, source_target_pairs={{0,1},{1,0},{2,3},{3,2},{4,5},{5,4},{6,7},{7,6},{8,9},{9,8},{10,11... | collective-permute-start | bytes 6152 | tf_op jit(solution)/shard_map/ppermute | solution.py:612
  32.9 25.4 %collective-permute-start.17 = (bf16[3,192,768]{2,1,0:T(8,128)(2,1)}, bf16[3,192,768]{2,1,0:T(8,128)(2,1)}, u32[]{:S(2)}, u32[]{:S(2)}) collective-permute-start(bf16[3,192,768]{2,1,0:T(8,128)(2,1)} %collective-permute-done.16.refs_20_), channel_id=1, source_target_pairs={{0,2},{2,0},{4,6},{6,4},{8,10},{10,8},{12,14},{14,12},{16,18},{18,... | collective-permute-start | bytes 2654216 | tf_op jit(solution)/shard_map/ppermute | solution.py:608
  37.6 11.4 %collective-permute-start.11 = (bf16[1,136,768]{2,1,0:T(8,128)(2,1)}, bf16[1,136,768]{2,1,0:T(8,128)(2,1)}, u32[]{:S(2)}, u32[]{:S(2)}) collective-permute-start(bf16[1,136,768]{2,1,0:T(8,128)(2,1)} %collective-permute-done.3.refs_4_), channel_id=1, source_target_pairs={{0,2},{2,0},{4,6},{6,4},{8,10},{10,8},{12,14},{14,12},{16,18},{18,... | collective-permute-start | bytes 626696 | tf_op jit(solution)/shard_map/ppermute | solution.py:608
  56.5 21.3 %collective-permute-start.18 = (bf16[3,192,768]{2,1,0:T(8,128)(2,1)S(1)}, bf16[3,192,768]{2,1,0:T(8,128)(2,1)S(1)}, u32[]{:S(2)}, u32[]{:S(2)}) collective-permute-start(bf16[3,192,768]{2,1,0:T(8,128)(2,1)S(1)} %pad_maximum_fusion.4), channel_id=1, source_target_pairs={{0,1},{1,0},{2,3},{3,2},{4,5},{5,4},{6,7},{7,6},{8,9},{9,8},{10,11... | collective-permute-start | bytes 2654216 | tf_op jit(solution)/shard_map/ppermute | solution.py:612
  57.3 51.1 %collective-permute-start.20 = (bf16[128,768]{1,0:T(8,128)(2,1)S(1)}, bf16[128,768]{1,0:T(8,128)(2,1)S(1)}, u32[]{:S(2)}, u32[]{:S(2)}) collective-permute-start(bf16[128,768]{1,0:T(8,128)(2,1)S(1)} %bitcast.115), channel_id=1, source_target_pairs={{0,1},{1,0},{2,3},{3,2},{4,5},{5,4},{6,7},{7,6},{8,9},{9,8},{10,11... | collective-permute-start | bytes 589832 | tf_op jit(solution)/shard_map/ppermute | solution.py:612
  77.9 20.3 %collective-permute-start.19 = (bf16[3,192,768]{2,1,0:T(8,128)(2,1)S(1)}, bf16[3,192,768]{2,1,0:T(8,128)(2,1)S(1)}, u32[]{:S(2)}, u32[]{:S(2)}) collective-permute-start(bf16[3,192,768]{2,1,0:T(8,128)(2,1)S(1)} %collective-permute-done.18.got_ref), channel_id=1, source_target_pairs={{0,2},{2,0},{4,6},{6,4},{8,10},{10,8},{12,14},{14,12},{16,18},{18,... | collective-permute-start | bytes 2654216 | tf_op jit(solution)/shard_map/ppermute | solution.py:608
  123.4 11.8 %collective-permute-start.28 = (bf16[1,128,896]{2,1,0:T(8,128)(2,1)}, bf16[1,128,896]{2,1,0:T(8,128)(2,1)}, u32[]{:S(2)}, u32[]{:S(2)}) collective-permute-start(bf16[1,128,896]{2,1,0:T(8,128)(2,1)} %bitcast.21), channel_id=1, source_target_pairs={{0,16},{2,18},{4,20},{6,22},{8,24},{10,26},{12,28},{14,30},{16,0},... | collective-permute-start | bytes 688136 | tf_op jit(solution)/shard_map/ppermute | solution.py:608
  135.2 177.1 %all-gather.2.cloned.1.call-start = ((), (), s32[]{:S(2)}) async-start(), calls=%async_computation.2 | async-start | bytes 5640192 | tf_op jit(solution)/shard_map/all_gather | solution.py:888
  136.1 20.8 %collective-permute-start.26 = (bf16[1,128,896]{2,1,0:T(8,128)(2,1)}, bf16[1,128,896]{2,1,0:T(8,128)(2,1)}, u32[]{:S(2)}, u32[]{:S(2)}) collective-permute-start(bf16[1,128,896]{2,1,0:T(8,128)(2,1)} %bitcast.21), channel_id=1, source_target_pairs={{0,8},{2,10},{4,12},{6,14},{8,0},{10,2},{12,4},{14,6},{16,24},{18,... | collective-permute-start | bytes 688136 | tf_op jit(solution)/shard_map/ppermute | solution.py:608
  139.2 19.3 %collective-permute-start.25 = (bf16[1,128,896]{2,1,0:T(8,128)(2,1)}, bf16[1,128,896]{2,1,0:T(8,128)(2,1)}, u32[]{:S(2)}, u32[]{:S(2)}) collective-permute-start(bf16[1,128,896]{2,1,0:T(8,128)(2,1)} %bitcast.21), channel_id=1, source_target_pairs={{0,4},{2,6},{4,0},{6,2},{8,12},{10,14},{12,8},{14,10},{16,20},{18,... | collective-permute-start | bytes 688136 | tf_op jit(solution)/shard_map/ppermute | solution.py:608
  140.4 11.7 %collective-permute-start.24 = (bf16[1,128,896]{2,1,0:T(8,128)(2,1)}, bf16[1,128,896]{2,1,0:T(8,128)(2,1)}, u32[]{:S(2)}, u32[]{:S(2)}) collective-permute-start(bf16[1,128,896]{2,1,0:T(8,128)(2,1)} %bitcast.21), channel_id=1, source_target_pairs={{0,24},{2,26},{4,28},{6,30},{8,16},{10,18},{12,20},{14,22},{16,8},... | collective-permute-start | bytes 688136 | tf_op jit(solution)/shard_map/ppermute | solution.py:608
  154.7 15.5 %collective-permute-start.32 = (bf16[1,128,896]{2,1,0:T(8,128)(2,1)}, bf16[1,128,896]{2,1,0:T(8,128)(2,1)}, u32[]{:S(2)}, u32[]{:S(2)}) collective-permute-start(bf16[1,128,896]{2,1,0:T(8,128)(2,1)} %bitcast.21), channel_id=1, source_target_pairs={{0,2},{2,0},{4,6},{6,4},{8,10},{10,8},{12,14},{14,12},{16,18},{18,... | collective-permute-start | bytes 688136 | tf_op jit(solution)/shard_map/ppermute | solution.py:608
  156.9 14.6 %collective-permute-start.38 = (bf16[1,128,896]{2,1,0:T(8,128)(2,1)}, bf16[1,128,896]{2,1,0:T(8,128)(2,1)}, u32[]{:S(2)}, u32[]{:S(2)}) collective-permute-start(bf16[1,128,896]{2,1,0:T(8,128)(2,1)} %collective-permute-done.24), channel_id=1, source_target_pairs={{0,2},{2,0},{4,6},{6,4},{8,10},{10,8},{12,14},{14,12},{16,18},{18,... | collective-permute-start | bytes 688136 | tf_op jit(solution)/shard_map/ppermute | solution.py:608
  156.9 15.0 %collective-permute-start.27 = (bf16[1,128,896]{2,1,0:T(8,128)(2,1)}, bf16[1,128,896]{2,1,0:T(8,128)(2,1)}, u32[]{:S(2)}, u32[]{:S(2)}) collective-permute-start(bf16[1,128,896]{2,1,0:T(8,128)(2,1)} %collective-permute-done.26), channel_id=1, source_target_pairs={{0,4},{2,6},{4,0},{6,2},{8,12},{10,14},{12,8},{14,10},{16,20},{18,... | collective-permute-start | bytes 688136 | tf_op jit(solution)/shard_map/ppermute | solution.py:608
  158.5 12.9 %collective-permute-start.33 = (bf16[1,128,896]{2,1,0:T(8,128)(2,1)}, bf16[1,128,896]{2,1,0:T(8,128)(2,1)}, u32[]{:S(2)}, u32[]{:S(2)}) collective-permute-start(bf16[1,128,896]{2,1,0:T(8,128)(2,1)} %collective-permute-done.25), channel_id=1, source_target_pairs={{0,2},{2,0},{4,6},{6,4},{8,10},{10,8},{12,14},{14,12},{16,18},{18,... | collective-permute-start | bytes 688136 | tf_op jit(solution)/shard_map/ppermute | solution.py:608
  159.3 12.7 %collective-permute-start.30 = (bf16[1,128,896]{2,1,0:T(8,128)(2,1)}, bf16[1,128,896]{2,1,0:T(8,128)(2,1)}, u32[]{:S(2)}, u32[]{:S(2)}) collective-permute-start(bf16[1,128,896]{2,1,0:T(8,128)(2,1)} %collective-permute-done.28), channel_id=1, source_target_pairs={{0,4},{2,6},{4,0},{6,2},{8,12},{10,14},{12,8},{14,10},{16,20},{18,... | collective-permute-start | bytes 688136 | tf_op jit(solution)/shard_map/ppermute | solution.py:608
  175.2 23.7 %collective-permute-start.40 = (bf16[128,384]{1,0:T(8,128)(2,1)S(1)}, bf16[128,384]{1,0:T(8,128)(2,1)S(1)}, u32[]{:S(2)}, u32[]{:S(2)}) collective-permute-start(bf16[128,384]{1,0:T(8,128)(2,1)S(1)} %get-tuple-element.136), channel_id=1, source_target_pairs={{0,1},{1,0},{2,3},{3,2},{4,5},{5,4},{6,7},{7,6},{8,9},{9,8},{10,11... | collective-permute-start | bytes 294920 | tf_op jit(solution)/shard_map/ppermute | solution.py:612
  175.5 23.3 %collective-permute-start.41 = (bf16[128,768]{1,0:T(8,128)(2,1)S(1)}, bf16[128,768]{1,0:T(8,128)(2,1)}, u32[]{:S(2)}, u32[]{:S(2)}) collective-permute-start(bf16[128,768]{1,0:T(8,128)(2,1)S(1)} %get-tuple-element.80), channel_id=1, source_target_pairs={{0,1},{1,0},{2,3},{3,2},{4,5},{5,4},{6,7},{7,6},{8,9},{9,8},{10,11... | collective-permute-start | bytes 589832 | tf_op jit(solution)/shard_map/ppermute | solution.py:612
  197.3 10.6 %collective-permute-start.42 = (bf16[128,1536]{1,0:T(8,128)(2,1)}, bf16[128,1536]{1,0:T(8,128)(2,1)}, u32[]{:S(2)}, u32[]{:S(2)}) collective-permute-start(bf16[128,1536]{1,0:T(8,128)(2,1)} %constant_dynamic-update-slice_fusion.8), channel_id=1, source_target_pairs={{0,1},{1,0},{2,3},{3,2},{4,5},{5,4},{6,7},{7,6},{8,9},{9,8},{10,11... | collective-permute-start | bytes 1179656 | tf_op jit(solution)/shard_map/ppermute | solution.py:612
  223.7 10.7 %collective-permute-start.45 = (bf16[4,80,768]{2,1,0:T(8,128)(2,1)}, bf16[4,80,768]{2,1,0:T(8,128)(2,1)}, u32[]{:S(2)}, u32[]{:S(2)}) collective-permute-start(bf16[4,80,768]{2,1,0:T(8,128)(2,1)} %constant_dynamic-slice_fusion.4), channel_id=1, source_target_pairs={{0,4},{2,6},{4,0},{6,2},{8,12},{10,14},{12,8},{14,10},{16,20},{18,... | collective-permute-start | bytes 1474568 | tf_op jit(solution)/shard_map/ppermute | solution.py:608
  238.9 11.0 %collective-permute-start.48 = (bf16[1,80,768]{2,1,0:T(8,128)(2,1)}, bf16[1,80,768]{2,1,0:T(8,128)(2,1)}, u32[]{:S(2)}, u32[]{:S(2)}) collective-permute-start(bf16[1,80,768]{2,1,0:T(8,128)(2,1)} %get-tuple-element.133), channel_id=1, source_target_pairs={{0,24},{2,26},{4,28},{6,30},{8,16},{10,18},{12,20},{14,22},{16,8},... | collective-permute-start | bytes 368648 | tf_op jit(solution)/shard_map/ppermute | solution.py:608
  240.9 14.8 %collective-permute-start.47 = (bf16[1,80,768]{2,1,0:T(8,128)(2,1)S(1)}, bf16[1,80,768]{2,1,0:T(8,128)(2,1)}, u32[]{:S(2)}, u32[]{:S(2)}) collective-permute-start(bf16[1,80,768]{2,1,0:T(8,128)(2,1)S(1)} %get-tuple-element.134), channel_id=1, source_target_pairs={{0,16},{2,18},{4,20},{6,22},{8,24},{10,26},{12,28},{14,30},{16,0},... | collective-permute-start | bytes 368648 | tf_op jit(solution)/shard_map/ppermute | solution.py:608
  256.8 13.1 %collective-permute-start.49 = (bf16[1,80,768]{2,1,0:T(8,128)(2,1)S(1)}, bf16[1,80,768]{2,1,0:T(8,128)(2,1)}, u32[]{:S(2)}, u32[]{:S(2)}) collective-permute-start(bf16[1,80,768]{2,1,0:T(8,128)(2,1)S(1)} %add_convert_fusion.2), channel_id=1, source_target_pairs={{0,8},{2,10},{4,12},{6,14},{8,0},{10,2},{12,4},{14,6},{16,24},{18,... | collective-permute-start | bytes 368648 | tf_op jit(solution)/shard_map/ppermute | solution.py:608
  259.0 12.2 %collective-permute-start.50 = (bf16[1,80,768]{2,1,0:T(8,128)(2,1)S(1)}, bf16[1,80,768]{2,1,0:T(8,128)(2,1)}, u32[]{:S(2)}, u32[]{:S(2)}) collective-permute-start(bf16[1,80,768]{2,1,0:T(8,128)(2,1)S(1)} %add_convert_fusion.2), channel_id=1, source_target_pairs={{0,16},{2,18},{4,20},{6,22},{8,24},{10,26},{12,28},{14,30},{16,0},... | collective-permute-start | bytes 368648 | tf_op jit(solution)/shard_map/ppermute | solution.py:608
  260.2 24.2 %collective-permute-start.51 = (bf16[1,80,768]{2,1,0:T(8,128)(2,1)S(1)}, bf16[1,80,768]{2,1,0:T(8,128)(2,1)}, u32[]{:S(2)}, u32[]{:S(2)}) collective-permute-start(bf16[1,80,768]{2,1,0:T(8,128)(2,1)S(1)} %add_convert_fusion.2), channel_id=1, source_target_pairs={{0,24},{2,26},{4,28},{6,30},{8,16},{10,18},{12,20},{14,22},{16,8},... | collective-permute-start | bytes 368648 | tf_op jit(solution)/shard_map/ppermute | solution.py:608
  286.4 10.3 %collective-permute-start.52 = (bf16[4,80,768]{2,1,0:T(8,128)(2,1)}, bf16[4,80,768]{2,1,0:T(8,128)(2,1)}, u32[]{:S(2)}, u32[]{:S(2)}) collective-permute-start(bf16[4,80,768]{2,1,0:T(8,128)(2,1)} %maximum_select_fusion.5), channel_id=1, source_target_pairs={{0,4},{2,6},{4,0},{6,2},{8,12},{10,14},{12,8},{14,10},{16,20},{18,... | collective-permute-start | bytes 1474568 | tf_op jit(solution)/shard_map/ppermute | solution.py:608
  289.4 13.4 %collective-permute-start.23 = (bf16[128,768]{1,0:T(8,128)(2,1)S(1)}, bf16[128,768]{1,0:T(8,128)(2,1)S(1)}, u32[]{:S(2)}, u32[]{:S(2)}) collective-permute-start(bf16[128,768]{1,0:T(8,128)(2,1)S(1)} %slice.214), channel_id=1, source_target_pairs={{0,1},{1,0},{2,3},{3,2},{4,5},{5,4},{6,7},{7,6},{8,9},{9,8},{10,11... | collective-permute-start | bytes 589832 | tf_op jit(solution)/shard_map/ppermute | solution.py:612
  (74 other events, 793.0 us)
Sparse Core Ops, SparseCore 0:
  135.4 81.9 reduce-scatter.1
  222.9 67.2 all-gather.1
where the time goes:
time: 330 us; the launch traced here: 328 us
  waiting for transfers between devices  101 us (31%)
  Pallas kernels  78.3 us (24%)
  starting transfers between devices  55.1 us (17%)
  local copies, waits for them, and re-layouts  35.8 us (11%)
  matrix products  25.1 us (8%)
  other arithmetic  17.5 us (5%)
  between operations  14.9 us (5%)
    ppermute x42, waiting for transfers between devices, swap_ctx(): return lax.ppermute(values, 'ctx', [(i, i ^ distance) for i in range(size)])  65.7 us
    ppermute x42, starting transfers between devices, swap_ctx(): return lax.ppermute(values, 'ctx', [(i, i ^ distance) for i in range(size)])  48.4 us
    ppermute x13, waiting for transfers between devices, swap_pair(): return lax.ppermute(values, 'fsdp', [(0, 1), (1, 0)])  35.4 us
    pallas_call x1, Pallas kernels, attend(): pl.pallas_call(functools.partial(attend_kernel, tile), grid=(pairs, n_chu...  17.2 us
    pallas_call x1, Pallas kernels, project(): pl.pallas_call(functools.partial(project_kernel, count, total, seqs), gri...  16.7 us
    pallas_call x1, Pallas kernels, key_back(): pl.pallas_call(functools.partial(key_back_kernel, count), grid=(pairs, n_...  15.8 us
    unnamed x113, local copies, waits for them, and re-layouts  15.1 us
    pallas_call x1, Pallas kernels, query_back(): pl.pallas_call(functools.partial(query_back_kernel, tile), grid=(pairs, n...  10.7 us
  transfers between devices with their start and end apart: 57, of which 23 were waited for; matrix products, arithmetic and copies ran while one was open for 19% of the time, Pallas kernels for 20%

commit v1 on v0

--- a/solution.py
+++ b/solution.py
@@ -7,11 +7,12 @@
 from jax.sharding import PartitionSpec as P
 
 BUCKETS = 32
-PIECES = 16
+PIECES = 8
 EPS = 1e-06
 NEG = -1000000000.0
 THRESHOLDS = (1, 2, 3, 4, 5, 6, 7, 8, 12, 16, 23, 32, 46, 64, 91)
 VMEM_BYTES = 50 * 1024 * 1024
+VMEM_MOST = 63 * 1024 * 1024
 
 
 def cost_of(micros):
@@ -50,25 +51,9 @@
     out_ref[j, pl.ds(pl.multiple_of(other + (1 - spot_ref[1]) * part, 64), part), :] = more
 
 
-def project_kernel(count, total, seqs, spot_ref, *refs):
-    pieces, refs = refs[:PIECES], refs[PIECES:]
-    gain_ref, wq_ref, wk_ref, wv_ref, got_ref, more_ref = refs[:6]
-    made_ref, idx_ref, normed_ref, full_ref, rows_scr, place_scr, own_scr = refs[6:]
-    width = gain_ref.shape[1]
-    rows = normed_ref.shape[0]
-    outer, inner = pl.program_id(0), pl.program_id(1)
-
-    for group in range(PIECES // count):
-
-        @pl.when(inner == group)
-        def _():
-            for j in range(count):
-                held = pieces[group * count + j][0]
-                rows_scr[j * rows : (j + 1) * rows, :] = held[:rows]
-                place_scr[j : j + 1, :] = held[rows:].astype(jnp.float32)[:1, : 2 * rows]
-
-    spots = place_scr[...]
-    spots = spots[:, :rows] * 128.0 + spots[:, rows:]
+def marks_of(places, total, seqs, spot_ref):
+    rows = places.shape[1] // 2
+    spots = places[:, :rows] * 128.0 + places[:, rows:]
     end = 0
     begin, segment = jnp.zeros_like(spots), jnp.zeros_like(spots)
     for j in range(seqs):
@@ -76,13 +61,35 @@
         passed = spots >= end.astype(jnp.float32)
         begin = jnp.where(passed, end.astype(jnp.float32), begin)
         segment = jnp.where(passed, segment + 1.0, segment)
-    marks = spots - begin + segment * (2.0 * total)
-
-    @pl.when((outer == 0) & (inner == 0))
-    def _():
-        own_scr[...] = marks[:1, :]
-        for j, ref in enumerate((wq_ref, wk_ref, wv_ref)):
-            fill_rows(full_ref, j, ref[...], got_ref[j], more_ref[j], spot_ref)
+    return spots - begin + segment * (2.0 * total)
+
+
+def project_kernel(count, total, seqs, first, spot_ref, *refs):
+    pieces, refs = refs[:PIECES], refs[PIECES:]
+    if first:
+        gain_ref, place_ref, wq_ref, wk_ref, wv_ref, got_ref, more_ref = refs[:7]
+        made_ref, idx_ref, full_ref, normed_ref, rows_scr, place_scr = refs[7:]
+    else:
+        gain_ref, place_ref, full_ref, made_ref, idx_ref, rows_scr, place_scr = refs
+    width = gain_ref.shape[1]
+    rows = idx_ref.shape[2]
+    outer, inner = pl.program_id(0), pl.program_id(1)
+
+    for group in range(PIECES // count):
+
+        @pl.when(inner == group)
+        def _():
+            for j in range(count):
+                held = pieces[group * count + j][0]
+                rows_scr[j * rows : (j + 1) * rows, :] = held[:rows]
+                place_scr[j : j + 1, :] = held[rows:].astype(jnp.float32)[:1, : 2 * rows]
+
+    if first:
+
+        @pl.when((outer == 0) & (inner == 0))
+        def _():
+            for j, ref in enumerate((wq_ref, wk_ref, wv_ref)):
+                fill_rows(full_ref, j, ref[...], got_ref[j], more_ref[j], spot_ref)
 
     values = rows_scr[...].astype(jnp.float32)
     inverse = lax.rsqrt(jnp.mean(values * values, axis=1, keepdims=True) + EPS)
@@ -92,13 +99,16 @@
         made = jnp.dot(normed, full_ref[j], preferred_element_type=jnp.float32)
         made_ref[:, :, j * width : (j + 1) * width] = made.astype(jnp.bfloat16).reshape(shape)
 
-    @pl.when((outer == 0) & (inner == 0))
-    def _():
-        normed_ref[...] = normed[:rows]
-
-    turned = jnp.transpose(marks)
+    if first:
+
+        @pl.when((outer == 0) & (inner == 0))
+        def _():
+            normed_ref[...] = normed[:rows]
+
+    own = marks_of(place_ref[...].astype(jnp.float32)[:1, : 2 * rows], total, seqs, spot_ref)
+    turned = jnp.transpose(marks_of(place_scr[...], total, seqs, spot_ref))
     for j in range(count):
-        offset = turned[:, j : j + 1] - own_scr[...]
+        offset = turned[:, j : j + 1] - own
         distance = jnp.abs(offset)
         bucket = jnp.where(offset > 0, BUCKETS // 2, 0)
         for threshold in THRESHOLDS:
@@ -106,48 +116,51 @@
         idx_ref[j] = jnp.where(distance >= total, BUCKETS, bucket)
 
 
-def project(spot, pieces, gain, weights, got, more, rows, total, seqs, count=4):
+def project(spot, pieces, gain, places, weights, rows, total, seqs, count=4):
     devices, tall, width = pieces[0].shape
-    held, part = weights[0].shape[0], got.shape[1]
-    fixed = lambda i, j, spot: (0, 0)
-    fixed3 = lambda i, j, spot: (0, 0, 0)
+    first = len(weights) > 1
+    fixed = lambda rank: (lambda i, j, spot: (0,) * rank)
     moving = lambda i, j, spot: (j, i, 0)
+    outputs = [
+        (
+            pl.BlockSpec((count, rows, 3 * width), moving),
+            jax.ShapeDtypeStruct((PIECES, devices * rows, 3 * width), jnp.bfloat16),
+        ),
+        (
+            pl.BlockSpec((count, rows, rows), moving),
+            jax.ShapeDtypeStruct((PIECES, devices * rows, rows), jnp.int32),
+        ),
+    ]
+    if first:
+        outputs += [
+            (
+                pl.BlockSpec((3, width, width), fixed(3)),
+                jax.ShapeDtypeStruct((3, width, width), jnp.bfloat16),
+            ),
+            (
+                pl.BlockSpec((rows, width), fixed(2)),
+                jax.ShapeDtypeStruct((rows, width), jnp.bfloat16),
+            ),
+        ]
+    operands = (gain, places) + tuple(weights)
     return pl.pallas_call(
-        functools.partial(project_kernel, count, total, seqs),
+        functools.partial(project_kernel, count, total, seqs, first),
         grid_spec=pltpu.PrefetchScalarGridSpec(
             num_scalar_prefetch=1,
             grid=(devices, PIECES // count),
             in_specs=[pl.BlockSpec((1, tall, width), lambda i, j, spot: (i, 0, 0))] * PIECES
-            + [
-                pl.BlockSpec((1, width), fixed),
-                pl.BlockSpec((held, width), fixed),
-                pl.BlockSpec((held, width), fixed),
-                pl.BlockSpec((held, width), fixed),
-                pl.BlockSpec((3, part, width), fixed3),
-                pl.BlockSpec((3, part, width), fixed3),
-            ],
-            out_specs=[
-                pl.BlockSpec((count, rows, 3 * width), moving),
-                pl.BlockSpec((count, rows, rows), moving),
-                pl.BlockSpec((rows, width), fixed),
-                pl.BlockSpec((3, width, width), fixed3),
-            ],
+            + [pl.BlockSpec(member.shape, fixed(member.ndim)) for member in operands],
+            out_specs=[spec for spec, _ in outputs],
             scratch_shapes=[
                 pltpu.VMEM((count * rows, width), jnp.bfloat16),
                 pltpu.VMEM((8, 2 * rows), jnp.float32),
-                pltpu.VMEM((1, rows), jnp.float32),
             ],
         ),
-        out_shape=[
-            jax.ShapeDtypeStruct((PIECES, devices * rows, 3 * width), jnp.bfloat16),
-            jax.ShapeDtypeStruct((PIECES, devices * rows, rows), jnp.int32),
-            jax.ShapeDtypeStruct((rows, width), jnp.bfloat16),
-            jax.ShapeDtypeStruct((3, width, width), jnp.bfloat16),
-        ],
+        out_shape=[shape for _, shape in outputs],
         compiler_params=pltpu.CompilerParams(vmem_limit_bytes=VMEM_BYTES),
         cost_estimate=cost_of(0.7 * PIECES * devices),
         name="project",
-    )(spot, *pieces, gain, *weights, got, more)
+    )(spot, *pieces, *operands)
 
 
 def close_kernel(spot_ref, attn_ref, x_ref, gain_ref, w_ref, got_ref, more_ref, resid_ref, normed_ref, attn_b_ref, full_ref):
@@ -279,8 +292,9 @@
 
 def unpack_kernel(tall, spot_ref, near_ref, far_ref, *out_refs):
     values = jnp.where(pl.program_id(0) == 0, near_ref[...], far_ref[...]).astype(jnp.float32)
-    for j, ref in enumerate(out_refs):
+    for j, ref in enumerate(out_refs[:-1]):
         ref[...] = values[:, j * tall : (j + 1) * tall, :]
+    out_refs[-1][...] = values[:, (len(out_refs) - 1) * tall :, :128]
 
 
 def unpack(spot, near, far, tall, outputs):
@@ -304,9 +318,11 @@
                     (step, high, width), lambda j, i, spot: (jnp.where(j == 0, 0, i), 0, 0)
                 ),
             ],
-            out_specs=[pl.BlockSpec((step, tall, width), place)] * outputs,
+            out_specs=[pl.BlockSpec((step, tall, width), place)] * outputs
+            + [pl.BlockSpec((step, high - outputs * tall, 128), place)],
         ),
-        out_shape=[jax.ShapeDtypeStruct((2 * half, tall, width), jnp.float32)] * outputs,
+        out_shape=[jax.ShapeDtypeStruct((2 * half, tall, width), jnp.float32)] * outputs
+        + [jax.ShapeDtypeStruct((2 * half, high - outputs * tall, 128), jnp.float32)],
         compiler_params=pltpu.CompilerParams(vmem_limit_bytes=VMEM_BYTES),
         cost_estimate=cost_of(4),
         name="unpack",
@@ -330,7 +346,7 @@
 
 def spread(spot, full, tall_ff, tall):
     size, high, width = full.shape
-    step = 2
+    step = 4
     return pl.pallas_call(
         functools.partial(spread_kernel, tall_ff, tall),
         grid_spec=pltpu.PrefetchScalarGridSpec(
@@ -354,7 +370,11 @@
     )(spot, full)
 
 
-def attend_kernel(tile, q_ref, k_ref, v_ref, idx_ref, tab_ref, o_ref, lse_ref, m_out, p_ref, s_scr, m_scr, l_scr, acc_scr):
+def attend_kernel(tile, first, q_ref, k_ref, v_ref, idx_ref, tab_ref, *refs):
+    if first:
+        outs, m_out, p_ref, s_scr, m_scr, l_scr, acc_scr = refs[:3], *refs[3:]
+    else:
+        kept, outs, m_out, p_ref, s_scr, m_scr, l_scr, acc_scr = refs[:3], refs[3:5], *refs[5:]
     chunk, n_chunks = pl.program_id(1), pl.num_programs(1)
     rows = q_ref.shape[0]
     half = q_ref.shape[1] // 2
@@ -362,9 +382,14 @@
 
     @pl.when(chunk == 0)
     def _():
-        m_scr[...] = jnp.full_like(m_scr, -3.0e38)
-        l_scr[...] = jnp.zeros_like(l_scr)
-        acc_scr[...] = jnp.zeros_like(acc_scr)
+        if first:
+            m_scr[...] = jnp.full_like(m_scr, -3.0e38)
+            l_scr[...] = jnp.zeros_like(l_scr)
+            acc_scr[...] = jnp.zeros_like(acc_scr)
+        else:
+            m_scr[...] = kept[0][0]
+            l_scr[...] = kept[1][0]
+            acc_scr[...] = kept[2][0]
 
     q_cat = pair_rows(q_ref[...], half)
     m_old = m_scr[...]
@@ -398,19 +423,46 @@
 
     @pl.when(chunk == n_chunks - 1)
     def _():
-        lse_ref[0] = m_new + jnp.log(l_new)
-        o_ref[...] = jnp.transpose(pair_blocks(acc / l_new, half, rows))
-
-
-def attend(made, index, table, chunk_keys, tile=512):
+        if first:
+            outs[0][0], outs[1][0], outs[2][0] = m_new, l_new, acc
+        else:
+            outs[0][...] = jnp.transpose(pair_blocks(acc / l_new, half, rows))
+            outs[1][0] = m_new + jnp.log(l_new)
+
+
+def attend(made_own, made, index, table, chunk_keys, kept=None, tile=512):
     total, rows = index.shape
     width = made.shape[1] // 3
     heads = table.shape[0] * 2
     pairs = table.shape[0]
     wide = width // pairs
     n_chunks = total // chunk_keys
+    first = kept is None
+    line = (
+        pl.BlockSpec((1, 1, 2 * rows), lambda p, c: (p, 0, 0)),
+        jax.ShapeDtypeStruct((pairs, 1, 2 * rows), jnp.float32),
+    )
+    square = (
+        pl.BlockSpec((1, wide, 2 * rows), lambda p, c: (p, 0, 0)),
+        jax.ShapeDtypeStruct((pairs, wide, 2 * rows), jnp.float32),
+    )
+    result = (
+        pl.BlockSpec((rows, wide), lambda p, c: (0, p)),
+        jax.ShapeDtypeStruct((rows, width), jnp.float32),
+    )
+    outputs = [line, line, square] if first else [result, line]
+    outputs += [
+        (
+            pl.BlockSpec((1, 1, 1, 2 * rows), lambda p, c: (p, c, 0, 0)),
+            jax.ShapeDtypeStruct((pairs, n_chunks, 1, 2 * rows), jnp.float32),
+        ),
+        (
+            pl.BlockSpec((2, chunk_keys, rows), lambda p, c: (p, c, 0)),
+            jax.ShapeDtypeStruct((heads, total, rows), jnp.bfloat16),
+        ),
+    ]
     return pl.pallas_call(
-        functools.partial(attend_kernel, tile),
+        functools.partial(attend_kernel, tile, first),
         grid=(pairs, n_chunks),
         in_specs=[
             pl.BlockSpec((rows, wide), lambda p, c: (0, p)),
@@ -418,19 +470,10 @@
             pl.BlockSpec((chunk_keys, wide), lambda p, c: (c, 2 * pairs + p)),
             pl.BlockSpec((chunk_keys, rows), lambda p, c: (c, 0)),
             pl.BlockSpec((1, 2, 128), lambda p, c: (p, 0, 0)),
-        ],
-        out_specs=[
-            pl.BlockSpec((rows, wide), lambda p, c: (0, p)),
-            pl.BlockSpec((1, 1, 2 * rows), lambda p, c: (p, 0, 0)),
-            pl.BlockSpec((1, 1, 1, 2 * rows), lambda p, c: (p, c, 0, 0)),
-            pl.BlockSpec((2, chunk_keys, rows), lambda p, c: (p, c, 0)),
-        ],
-        out_shape=[
-            jax.ShapeDtypeStruct((rows, width), jnp.float32),
-            jax.ShapeDtypeStruct((pairs, 1, 2 * rows), jnp.float32),
-            jax.ShapeDtypeStruct((pairs, n_chunks, 1, 2 * rows), jnp.float32),
-            jax.ShapeDtypeStruct((heads, total, rows), jnp.bfloat16),
-        ],
+        ]
+        + ([] if first else [line[0], line[0], square[0]]),
+        out_specs=[spec for spec, _ in outputs],
+        out_shape=[shape for _, shape in outputs],
         scratch_shapes=[
             pltpu.VMEM((chunk_keys, 2 * rows), jnp.float32),
             pltpu.VMEM((1, 2 * rows), jnp.float32),
@@ -440,31 +483,33 @@
         compiler_params=pltpu.CompilerParams(vmem_limit_bytes=VMEM_BYTES),
         cost_estimate=cost_of(0.008 * total),
         name="attend",
-    )(made, made, made, index, table)
-
-
-def query_back_kernel(tile, p_ref, v_ref, k_ref, da_ref, delta_ref, lse_ref, m_ref, ds_ref, dq_ref, acc_scr):
+    )(made_own, made, made, index, table, *([] if first else kept))
+
+
+def query_back_kernel(tile, *refs):
+    groups, refs = (refs[0:4], refs[4:8]), refs[8:]
+    da_ref, delta_ref, lse_ref, dq_ref, acc_scr = refs[:3] + refs[5:]
     chunk, n_chunks = pl.program_id(1), pl.num_programs(1)
     rows = da_ref.shape[0]
     half = da_ref.shape[1] // 2
-    keys = v_ref.shape[0]
 
     @pl.when(chunk == 0)
     def _():
         acc_scr[...] = jnp.zeros_like(acc_scr)
 
-    factor = jnp.exp(m_ref[0, 0] - lse_ref[0])
     delta = delta_ref[0]
     da_cat = pair_rows(da_ref[...], half)
     acc = acc_scr[...]
-    for t in range(keys // tile):
-        rng = slice(t * tile, (t + 1) * tile)
-        dp = dot_nt(v_ref[rng, :], da_cat)
-        p = jnp.concatenate([p_ref[0, rng, :], p_ref[1, rng, :]], axis=1).astype(jnp.float32)
-        ds = ((p * factor) * (dp - delta)).astype(jnp.bfloat16)
-        ds_ref[0, rng, :] = ds[:, :rows]
-        ds_ref[1, rng, :] = ds[:, rows:]
-        acc = acc + dot_tn(k_ref[rng, :], ds)
+    for (p_ref, v_ref, k_ref, m_ref), ds_ref in zip(groups, refs[3:5]):
+        factor = jnp.exp(m_ref[0, 0] - lse_ref[0])
+        for t in range(v_ref.shape[0] // tile):
+            rng = slice(t * tile, (t + 1) * tile)
+            dp = dot_nt(v_ref[rng, :], da_cat)
+            p = jnp.concatenate([p_ref[0, rng, :], p_ref[1, rng, :]], axis=1).astype(jnp.float32)
+            ds = ((p * factor) * (dp - delta)).astype(jnp.bfloat16)
+            ds_ref[0, rng, :] = ds[:, :rows]
+            ds_ref[1, rng, :] = ds[:, rows:]
+            acc = acc + dot_tn(k_ref[rng, :], ds)
     acc_scr[...] = acc
 
     @pl.when(chunk == n_chunks - 1)
@@ -472,43 +517,44 @@
         dq_ref[...] = jnp.transpose(pair_blocks(acc, half, rows)).astype(jnp.bfloat16)
 
 
-def query_back(probs, made, payload, delta, lse, lows, chunk_keys, tile=512):
-    heads, total, rows = probs.shape
+def query_back(probs, mades, lows, payload, delta, lse, chunk_keys, tile=512):
+    heads, total, rows = probs[0].shape
     pairs = heads // 2
-    width = made.shape[1] // 3
+    width = mades[0].shape[1] // 3
     wide = width // pairs
     n_chunks = total // chunk_keys
+    prob = pl.BlockSpec((2, chunk_keys, rows), lambda p, c: (p, c, 0))
+    line = pl.BlockSpec((1, 1, 2 * rows), lambda p, c: (p, 0, 0))
+    group = [
+        prob,
+        pl.BlockSpec((chunk_keys, wide), lambda p, c: (c, 2 * pairs + p)),
+        pl.BlockSpec((chunk_keys, wide), lambda p, c: (c, pairs + p)),
+        pl.BlockSpec((1, 1, 1, 2 * rows), lambda p, c: (p, c, 0, 0)),
+    ]
+    members = [(probs[j], mades[j], mades[j], lows[j]) for j in range(2)]
     return pl.pallas_call(
         functools.partial(query_back_kernel, tile),
         grid=(pairs, n_chunks),
-        in_specs=[
-            pl.BlockSpec((2, chunk_keys, rows), lambda p, c: (p, c, 0)),
-            pl.BlockSpec((chunk_keys, wide), lambda p, c: (c, 2 * pairs + p)),
-            pl.BlockSpec((chunk_keys, wide), lambda p, c: (c, pairs + p)),
-            pl.BlockSpec((rows, wide), lambda p, c: (0, p)),
-            pl.BlockSpec((1, 1, 2 * rows), lambda p, c: (p, 0, 0)),
-            pl.BlockSpec((1, 1, 2 * rows), lambda p, c: (p, 0, 0)),
-            pl.BlockSpec((1, 1, 1, 2 * rows), lambda p, c: (p, c, 0, 0)),
-        ],
-        out_specs=[
-            pl.BlockSpec((2, chunk_keys, rows), lambda p, c: (p, c, 0)),
-            pl.BlockSpec((rows, wide), lambda p, c: (0, p)),
-        ],
+        in_specs=group + group + [pl.BlockSpec((rows, wide), lambda p, c: (0, p)), line, line],
+        out_specs=[prob, prob, pl.BlockSpec((rows, wide), lambda p, c: (0, p))],
         out_shape=[
+            jax.ShapeDtypeStruct((heads, total, rows), jnp.bfloat16),
             jax.ShapeDtypeStruct((heads, total, rows), jnp.bfloat16),
             jax.ShapeDtypeStruct((rows, width), jnp.bfloat16),
         ],
         scratch_shapes=[pltpu.VMEM((wide, 2 * rows), jnp.float32)],
-        input_output_aliases={0: 0},
+        input_output_aliases={0: 0, 4: 1},
         compiler_params=pltpu.CompilerParams(vmem_limit_bytes=VMEM_BYTES),
-        cost_estimate=cost_of(0.005 * total),
+        cost_estimate=cost_of(0.01 * total),
         name="query_back",
-    )(probs, made, made, payload, delta, lse, lows)
+    )(*members[0], *members[1], payload, delta, lse)
 
 
 def key_back_kernel(count, *refs):
-    grads, auxes, refs = refs[:PIECES], refs[PIECES : 2 * PIECES], refs[2 * PIECES :]
-    q_ref, idx_ref, k_ref, v_ref, tab_ref, dk_ref, dv_ref, dk_scr, dv_scr = refs
+    n_pieces = 2 * PIECES
+    grads, auxes, refs = refs[:n_pieces], refs[n_pieces : 2 * n_pieces], refs[2 * n_pieces :]
+    q_refs, idx_refs, refs = refs[:2], refs[2:4], refs[4:]
+    k_ref, v_ref, tab_ref, out_ref, dk_scr, dv_scr = refs
     pair, chunk, n_chunks = pl.program_id(0), pl.program_id(1), pl.num_programs(1)
     rows = k_ref.shape[0]
     wide = k_ref.shape[1]
@@ -521,18 +567,19 @@
 
     lane = lax.broadcasted_iota(jnp.int32, (2 * rows, 128), 1)
     head = 2 * pair + (lax.broadcasted_iota(jnp.int32, (2 * rows, 128), 0) >= rows).astype(jnp.int32)
-    first = (lane >= 2 * head) & (lane < 2 * head + 2)
-    second = (lane >= 64 + 2 * head) & (lane < 64 + 2 * head + 2)
-    take_lse = jnp.where(first, -1.0, 0.0).astype(jnp.bfloat16)
-    take_delta = jnp.where(second, -1.0, 0.0).astype(jnp.bfloat16)
+    early = (lane >= 2 * head) & (lane < 2 * head + 2)
+    late = (lane >= 64 + 2 * head) & (lane < 64 + 2 * head + 2)
+    take_lse = jnp.where(early, -1.0, 0.0).astype(jnp.bfloat16)
+    take_delta = jnp.where(late, -1.0, 0.0).astype(jnp.bfloat16)
     k_cat = jnp.concatenate([pair_rows(k_ref[...], half), take_lse], axis=1)
     v_cat = jnp.concatenate([pair_rows(v_ref[...], half), take_delta], axis=1)
     dk, dv = dk_scr[...], dv_scr[...]
-    for t in range(0, PIECES, count):
+    for t in range(0, n_pieces, count):
+        group, at = t // PIECES, t % PIECES
         da = jnp.concatenate([ref[...] for ref in grads[t : t + count]], axis=0)
         aux = jnp.concatenate([ref[...] for ref in auxes[t : t + count]], axis=0)
-        q = q_ref[t : t + count].reshape(count * rows, wide)
-        index = idx_ref[t : t + count].reshape(count * rows, rows)
+        q = q_refs[group][at : at + count].reshape(count * rows, wide)
+        index = idx_refs[group][at : at + count].reshape(count * rows, rows)
         s = dot_nt(jnp.concatenate([q, aux], axis=1), k_cat)
         bias = jnp.concatenate(
             [bias_of(tab_ref[0, j : j + 1, :], index) for j in range(2)], axis=1
@@ -546,44 +593,35 @@
 
     @pl.when(chunk == n_chunks - 1)
     def _():
-        dk_ref[...] = jnp.transpose(pair_blocks(dk, half, rows)).astype(jnp.bfloat16)
-        dv_ref[...] = jnp.transpose(pair_blocks(dv, half, rows)).astype(jnp.bfloat16)
-
-
-def key_back(pieces, made, index, table, count=4):
-    rows = index.shape[2]
-    side, width = made.shape[1], made.shape[2] // 3
+        for j, acc in enumerate((dk, dv)):
+            out_ref[j] = jnp.transpose(pair_blocks(acc, half, rows)).astype(jnp.bfloat16)
+
+
+def key_back(pieces, mades, indexes, table, count=4):
+    rows = indexes[0].shape[2]
+    side, width = mades[0].shape[1], mades[0].shape[2] // 3
     pairs = table.shape[0]
     wide = width // pairs
     n_chunks = side // rows
     return pl.pallas_call(
         functools.partial(key_back_kernel, count),
         grid=(pairs, n_chunks),
-        in_specs=[pl.BlockSpec((rows, wide), lambda p, c: (c, p))] * PIECES
-        + [pl.BlockSpec((rows, 128), lambda p, c: (c, pairs))] * PIECES
+        in_specs=[pl.BlockSpec((rows, wide), lambda p, c: (c, p))] * len(pieces)
+        + [pl.BlockSpec((rows, 128), lambda p, c: (c, pairs))] * len(pieces)
+        + [pl.BlockSpec((PIECES, rows, wide), lambda p, c: (0, c, p))] * 2
+        + [pl.BlockSpec((PIECES, rows, rows), lambda p, c: (0, c, 0))] * 2
         + [
-            pl.BlockSpec((PIECES, rows, wide), lambda p, c: (0, c, p)),
-            pl.BlockSpec((PIECES, rows, rows), lambda p, c: (0, c, 0)),
-            pl.BlockSpec((rows, wide), lambda p, c: (0, pairs + p)),
-            pl.BlockSpec((rows, wide), lambda p, c: (0, 2 * pairs + p)),
+            pl.BlockSpec((None, rows, wide), lambda p, c: (0, 0, pairs + p)),
+            pl.BlockSpec((None, rows, wide), lambda p, c: (0, 0, 2 * pairs + p)),
             pl.BlockSpec((1, 2, 128), lambda p, c: (p, 0, 0)),
         ],
-        out_specs=[
-            pl.BlockSpec((rows, wide), lambda p, c: (0, p)),
-            pl.BlockSpec((rows, wide), lambda p, c: (0, p)),
-        ],
-        out_shape=[
-            jax.ShapeDtypeStruct((rows, width), jnp.bfloat16),
-            jax.ShapeDtypeStruct((rows, width), jnp.bfloat16),
-        ],
-        scratch_shapes=[
-            pltpu.VMEM((wide, 2 * rows), jnp.float32),
-            pltpu.VMEM((wide, 2 * rows), jnp.float32),
-        ],
-        compiler_params=pltpu.CompilerParams(vmem_limit_bytes=VMEM_BYTES),
+        out_specs=pl.BlockSpec((2, rows, wide), lambda p, c: (0, 0, p)),
+        out_shape=jax.ShapeDtypeStruct((2, rows, width), jnp.bfloat16),
+        scratch_shapes=[pltpu.VMEM((wide, 2 * rows), jnp.float32)] * 2,
+        compiler_params=pltpu.CompilerParams(vmem_limit_bytes=VMEM_MOST),
         cost_estimate=cost_of(15 * n_chunks),
         name="key_back",
-    )(*pieces, *pieces, made, index, made[0], made[0], table)
+    )(*pieces, *pieces, *mades, *indexes, mades[0], mades[0], table)
 
 
 def norm_back(values, inverse, scale_gain, grad_normed):
@@ -629,37 +667,36 @@
     return lax.optimization_barrier(members)
 
 
-def gather_group(block, ties=(None, None, None, None)):
+def gather_far(block):
     size = lax.axis_size("ctx")
     quarter = size // 4
-    ties = list(ties)
     block = block[None]
     distance = 2 * 2
     while distance < quarter:
         block = jnp.concatenate([block, swap_ctx(block, distance)], axis=0)
         distance *= 2
-    far = [swap_ctx(block, quarter * j) for j in (1, 2, 3)]
-    near = [block, swap_ctx(block, 2)]
-    for j in range(3):
-        if ties[j] is not None:
-            far[j], ties[j] = tied(far[j], ties[j])
-        near += [far[j], swap_ctx(far[j], 2)]
-    if ties[3] is not None:
-        near[-1], ties[3] = tied(near[-1], ties[3])
-    return near + [swap_ctx(piece, 1) for piece in near], ties
-
-
-def scatter_sum(blocks, tie):
+    return [block] + [swap_ctx(block, quarter * j) for j in (1, 2, 3)]
+
+
+def with_other_core(members):
+    return members + [swap_ctx(piece, 1) for piece in members]
+
+
+def scatter_sum(keep, send, tie):
     here, size = lax.axis_index("ctx"), lax.axis_size("ctx")
-    low, f32 = blocks.dtype, jnp.float32
-    distance = 1
-    while distance < size // 4:
+    f32, low, distance = jnp.float32, keep.dtype, 1
+    got = swap_ctx(send, distance)
+    while distance < size // 8:
+        blocks = (keep.astype(f32) + got.astype(f32)).astype(low)
+        distance *= 2
         mine = (here // distance) % 2
-        got = swap_ctx(part_of(blocks, 1 - mine, 2, 0), distance)
-        blocks = (part_of(blocks, mine, 2, 0).astype(f32) + got.astype(f32)).astype(low)
-        if distance == 1:
-            blocks, tie = tied(blocks, tie)
-        distance *= 2
+        send = part_of(blocks, 1 - mine, 2, 0)
+        if distance == 2:
+            send, tie = tied(send, tie)
+        got = swap_ctx(send, distance)
+        keep = part_of(blocks, mine, 2, 0)
+    blocks = (keep.astype(f32) + got.astype(f32)).astype(low)
+    distance *= 2
     mine = here // distance
     got = [swap_ctx(part_of(blocks, mine ^ j, 4, 0), distance * j) for j in (1, 2, 3)]
     added = part_of(blocks, mine, 4, 0).astype(f32) + sum(member.astype(f32) for member in got)
@@ -708,7 +745,7 @@
     total = size * rows
     half_ff = w_ff.shape[0]
     half_width = w_query.shape[0]
-    chunk_keys = min(total, 2048)
+    chunk_keys = min(total // 2, 1024)
 
     spot = jnp.concatenate(
         [jnp.stack([pair, lax.axis_index("ctx") % 2]).astype(jnp.int32), lengths[0]]
@@ -717,7 +754,9 @@
     dealt = dealing[0]
     place_row = jnp.concatenate([dealt // 128, dealt % 128]).astype(bf16)
     place_rows = jnp.pad(place_row[None], ((0, 7), (0, width - 2 * rows)))
-    pieces = gather_group(jnp.concatenate([tokens[0], place_rows], axis=0))[0]
+    far = gather_far(jnp.concatenate([tokens[0], place_rows], axis=0))
+    *far, above = tied(*far, swap_ctx(far[0], 2))
+    above = [above] + [swap_ctx(piece, 2) for piece in far[1:]]
 
     small = jnp.concatenate([gain_one, gain_two, rel_table.reshape(-1)])
     small = jnp.pad(small, (0, 1024 - small.shape[0])).reshape(8, 128)
@@ -729,8 +768,9 @@
     full_table = small_full[:, 2 * half_width : 2 * half_width + rel_table.size]
     full_table = full_table.reshape(2 * rel_table.shape[0], heads).astype(f32)
     got_one = sent_weights(w_query, w_key, w_value)
+    got_one, above[1] = tied(got_one, above[1])
     more_one = swap_ctx(got_one, 1)
-    pieces[4], w_out, w_in, cotangent = tied(pieces[4], w_out, w_in, cotangent)
+    more_one, w_out, w_in, cotangent = tied(more_one, w_out, w_in, cotangent)
     mine_in, other_in = (part_of(w_in, index, 2, 1) for index in (pair, 1 - pair))
     got_two = sent_weights(w_out, other_in[:, :width], other_in[:, width:])
     grad_out = cotangent[0]
@@ -744,21 +784,25 @@
         jnp.pad(tab, ((0, 0), (0, 128 - BUCKETS)), constant_values=NEG).reshape(pairs, 2, 128)
         for tab in (table_t, back_t)
     ]
-    made, index, normed_one, w_qkv = project(
-        spot,
-        pieces,
-        gain32_one[None],
-        (w_query, w_key, w_value),
-        got_one,
-        more_one,
-        rows,
-        total,
-        lengths.shape[1],
-    )
-    made, got_two = tied(made, got_two)
+    fixed = (rows, total, lengths.shape[1])
+    weights = (w_query, w_key, w_value, got_one, more_one)
+    gain_row = gain32_one[None]
+    made_one, index_one, w_qkv, normed_one = project(
+        spot, with_other_core(far[:2] + above[:2]), gain_row, place_rows, weights, *fixed
+    )
+    above[2], above[3], made_one = tied(above[2], above[3], made_one)
+    pieces = with_other_core(far[2:] + above[2:])
+    mades, indexes = [made_one.reshape(total // 2, -1)], [index_one.reshape(total // 2, rows)]
+    *kept, low_one, prob_one = attend(mades[0], mades[0], indexes[0], tables[0], chunk_keys)
+    pieces, kept, got_two = tied(pieces, kept, got_two)
     more_two = swap_ctx(got_two, 1)
-    flat_made, flat_index = made.reshape(total, 3 * width), index.reshape(total, rows)
-    attn_f32, lse, lows, probs = attend(flat_made, flat_index, tables[0], chunk_keys)
+    made_two, index_two = project(spot, pieces, gain_row, place_rows, (w_qkv,), *fixed)
+    mades.append(made_two.reshape(total // 2, -1))
+    indexes.append(index_two.reshape(total // 2, rows))
+    attn_f32, lse, low_two, prob_two = attend(
+        mades[0], mades[1], indexes[1], tables[0], chunk_keys, kept
+    )
+    lows, probs = (low_one, low_two), (prob_one, prob_two)
 
     resid, normed_two, attn_b, full_out = close(
         spot, attn_f32, tokens[0], gain32_two[None], w_out, got_two, more_two
@@ -783,7 +827,7 @@
     grad_pre = gate_pull(grad_active)[0].astype(bf16)
     grad_normed_part = jnp.einsum("tf,df->td", grad_pre, half_in, preferred_element_type=f32)
     payload, delta, grad_resid, grad_branch, grad_gain_two = branch(
-        grad_normed_part[:rows],
+        grad_normed_part,
         swap_pair(grad_normed_part[rows:].astype(bf16)),
         resid,
         grad_out,
@@ -830,36 +874,51 @@
     )
     ff_tall = ff_blocks.shape[1]
 
-    grad_scores, grad_q = query_back(
-        probs, flat_made, payload, delta.reshape(pairs, 1, 2 * rows), lse, lows, chunk_keys
-    )
-    one_hot = (flat_index[:, :, None] == jnp.arange(BUCKETS, dtype=jnp.int32)).astype(bf16)
-    grad_tab = jnp.einsum("hkq,kqb->hb", grad_scores, one_hot, preferred_element_type=f32)
-    grad_pieces, ties = gather_group(
-        payload, ((grad_ff_part, grad_in_part), ff_blocks, grad_q, grad_tab)
-    )
-    ff_blocks, grad_q, grad_tab = ties[1:]
+    far = gather_far(payload)
+    *far, above, ff_blocks, payload = tied(*far, swap_ctx(far[0], 2), ff_blocks, payload)
+    above = [above] + [swap_ctx(piece, 2) for piece in far[1:]]
+    above[1], payload = tied(above[1], payload)
+    *grad_scores, grad_q = query_back(
+        probs, mades, lows, payload, delta.reshape(pairs, 1, 2 * rows), lse, chunk_keys
+    )
+    above[1], above[2], above[3], grad_scores = tied(*above[1:], grad_scores)
+    pieces = with_other_core(far[:2] + above[:2]) + with_other_core(far[2:] + above[2:])
+    grad_tab = sum(
+        jnp.einsum(
+            "hkq,kqb->hb",
+            member,
+            (where[:, :, None] == jnp.arange(BUCKETS, dtype=jnp.int32)).astype(bf16),
+            preferred_element_type=f32,
+        )
+        for member, where in zip(grad_scores, indexes)
+    )
     ff_sum = lax.psum_scatter(
         ff_blocks.reshape(size * ff_tall, width), "ctx", scatter_dimension=0, tiled=True
     )
-    grad_k, grad_v = key_back(
-        [piece.reshape(-1, width + 128) for piece in grad_pieces], made, index, tables[1]
+    pieces[-1], grad_tab = tied(pieces[-1], grad_tab)
+    active, normed_one, grad_tab = tied(active, normed_one, grad_tab)
+    grads_kv = key_back(
+        ([payload] if size == 16 else [pieces[0].reshape(-1, width + 128)])
+        + [piece.reshape(-1, width + 128) for piece in pieces[1:]],
+        (made_one, made_two),
+        (index_one, index_two),
+        tables[1],
     )
     out_part = dot_f32(active, w_ff)
-    output = resid + out_part[:rows] + swap_pair(out_part[rows:].astype(bf16)).astype(f32)
-
-    grads_kv = jnp.concatenate([grad_k, grad_v], axis=1)
+    out_other = swap_pair(out_part[rows:].astype(bf16))
+    kv_other = swap_pair(grads_kv)
     normed_halves = halves(normed_one)
-    grad_q_part = by_rows(normed_halves, both(grad_q))
-    grad_kv_part = by_rows(normed_halves, both(grads_kv))
+    q_other = swap_pair(grad_q)
     inputs = tokens[0].astype(f32)
     inv_one = lax.rsqrt(jnp.mean(inputs * inputs, axis=1, keepdims=True) + EPS)
     grad_normed_one = sum(
         jnp.einsum("te,de->td", member, w_qkv[j], preferred_element_type=f32)
-        for j, member in enumerate((grad_q, grad_k, grad_v))
+        for j, member in enumerate((grad_q, grads_kv[0], grads_kv[1]))
     )
     grad_gain_one, grad_input_norm = norm_back(inputs, inv_one, gain32_one, grad_normed_one)
     grad_tokens = grad_resid + grad_input_norm
+    kv_other, out_other = tied(kv_other, out_other)
+    output = resid + out_part[:rows] + out_other.astype(f32)
 
     small_grads = jnp.concatenate(
         [
@@ -876,23 +935,27 @@
     small_blocks = jnp.pad(
         small_pair.astype(bf16).reshape(size, 1, each), ((0, 0), (0, 7), (0, width - each))
     )
-    qkv_sum, ff_sum = scatter_sum(
-        jnp.concatenate(
-            blocks_of(grad_q_part) + blocks_of(grad_kv_part) + [small_blocks], axis=1
-        ),
-        ff_sum,
-    )
+    rights = [jnp.concatenate([grad_q, q_other])] + [
+        jnp.concatenate([grads_kv[j], kv_other[j]]) for j in range(2)
+    ]
+
+    def core_blocks(side):
+        left = part_of(normed_halves, side, 2, 1)
+        made = [by_rows(left, right).reshape(size // 2, tall, width) for right in rights]
+        return jnp.concatenate(made + [part_of(small_blocks, side, 2, 0)], axis=1)
+
+    send = core_blocks(1 - spot[1])
+    qkv_sum, ff_sum = scatter_sum(core_blocks(spot[1]), send, ff_sum)
     first_in, last_in = tall_ff, tall_ff + 4 * tall
     moved = swap_pair(ff_sum[tall_ff + 2 * tall : last_in])
     ff_sum = jnp.concatenate([ff_sum[: tall_ff + 2 * tall], moved, ff_sum[last_in:]], axis=0)
     ff_full = lax.all_gather(ff_sum, "ctx", axis=0, tiled=True).reshape(size, ff_tall, width)
     near_sum, far_sum = gather_back(qkv_sum)
-    small_halves = [member[:, 3 * tall, :each].reshape(-1) for member in (near_sum, far_sum)]
-    small_mine = in_order(spot[1], *small_halves).astype(f32)
-    grad_qkv = [
-        member.reshape(half_width, width) for member in unpack(spot, near_sum, far_sum, tall, 3)
-    ]
+    *grad_qkv, small_mine = unpack(spot, near_sum, far_sum, tall, 3)
+    grad_qkv[0], ff_full = tied(grad_qkv[0], ff_full)
     grad_ff, grad_in, grad_out_w = spread(spot, ff_full, tall_ff, tall)
+    grad_qkv = [member.reshape(half_width, width) for member in grad_qkv]
+    small_mine = small_mine[:, 0, :each].reshape(-1)
     return (
         output.astype(bf16)[None],
         grad_tokens[None],

time: 330 us -> 310 us (0.939)
  local copies, waits for them, and re-layouts: 35.8 us -> 20.7 us
  other arithmetic: 17.5 us -> 7.23 us
  waiting for transfers between devices: 101 us -> 109 us
    ppermute x42, waiting for transfers between devices: 65.7 us -> 89.6 us  [swap_ctx(): return lax.ppermute(values, 'ctx', [(i, i ^ distance) for i in range(size)])]
    ppermute x13, waiting for transfers between devices: 35.4 us -> 13.6 us  [swap_pair(): return lax.ppermute(values, 'fsdp', [(0, 1), (1, 0)])]
    ppermute x42, starting transfers between devices: 48.4 us -> 40.9 us  [swap_ctx(): return lax.ppermute(values, 'ctx', [(i, i ^ distance) for i in range(size)])]
    unnamed x113 -> x128, local copies, waits for them, and re-layouts: 15.1 us -> 8.99 us
    reduce_scatter x1, waiting for transfers between devices: 0.02 us -> 5.27 us  [shards(): lax.psum_scatter(ff_blocks.reshape(size * ff_tall, width), 'ctx', scatter...]
    pallas_call x2 -> x4, Pallas kernels: 33.9 us -> 38.9 us  [the longest x2 20 us: attend(): pl.pallas_call(functools.partial(attend_kernel, tile, first), grid=(pairs...]
    ppermute x13, starting transfers between devices: 6.59 us -> 11.3 us  [swap_pair(): return lax.ppermute(values, 'fsdp', [(0, 1), (1, 0)])]
    select_n x7 -> x8, other arithmetic: 5.97 us -> 1.59 us  [in_order(): jnp.where(where == 0, jnp.concatenate([mine, other], axis=axis), jnp.conc...]
  transfers between devices with their start and end apart: 57 -> 57, of which waited for: 23 -> 22; matrix products, arithmetic and copies ran while one was open for 19% -> 13% of each run, Pallas kernels for 20% -> 22%
where the time goes in v1:
time: 310 us; the launch traced here: 309 us
  waiting for transfers between devices  109 us (35%)
  Pallas kernels  77.4 us (25%)
  starting transfers between devices  52.2 us (17%)
  matrix products  27.9 us (9%)
  local copies, waits for them, and re-layouts  20.7 us (7%)
  between operations  15.1 us (5%)
  other arithmetic  7.23 us (2%)
    ppermute x42, waiting for transfers between devices, swap_ctx(): return lax.ppermute(values, 'ctx', [(i, i ^ distance) for i in range(size)])  89.6 us
    ppermute x42, starting transfers between devices, swap_ctx(): return lax.ppermute(values, 'ctx', [(i, i ^ distance) for i in range(size)])  40.9 us
    pallas_call x2, Pallas kernels, attend(): pl.pallas_call(functools.partial(attend_kernel, tile, first), grid=(pairs...  20 us
    pallas_call x2, Pallas kernels, project(): pl.pallas_call(functools.partial(project_kernel, count, total, seqs, firs...  18.9 us
    pallas_call x1, Pallas kernels, key_back(): pl.pallas_call(functools.partial(key_back_kernel, count), grid=(pairs, n_...  15.9 us
    ppermute x13, waiting for transfers between devices, swap_pair(): return lax.ppermute(values, 'fsdp', [(0, 1), (1, 0)])  13.6 us
    ppermute x13, starting transfers between devices, swap_pair(): return lax.ppermute(values, 'fsdp', [(0, 1), (1, 0)])  11.3 us
    dot_general x2, matrix products, shards(): jnp.einsum('hkq,kqb->hb', member, (where[:, :, None] == jnp.arange(BUCKET...  9.4 us
  transfers between devices with their start and end apart: 57, of which 22 were waited for; matrix products, arithmetic and copies ran while one was open for 13% of the time, Pallas kernels for 22%

profile of v1, /device:TPU:11, one launch (start us, length us, event | category | flops | bytes accessed | tf_op | source)
XLA Modules:
  0.0 309.0 jit_solution(12145781838524441876)
XLA Ops:
  11.8 2.5 collective-permute-start.1
  15.8 2.7 collective-permute-done.refs_1_
  18.4 4.6 %collective-permute-done.1.refs_0_ = bf16[1,136,768]{2,1,0:T(8,128)(2,1)S(1)} collective-permute-done((bf16[1,136,768]{2,1,0:T(8,128)(2,1)S(1)}, bf16[1,136,768]{2,1,0:T(8,128)(2,1)S(1)}, u32[]{:S(2)}, u32[]{:S(2)}) %collective-permute-start.1) | collective-permute-done | bytes 208928 | tf_op jit(solution)/shard_map/ppermute | solution.py:646
  23.0 9.0 %collective-permute-done.2.refs_1_ = bf16[1,136,768]{2,1,0:T(8,128)(2,1)S(1)} collective-permute-done((bf16[1,136,768]{2,1,0:T(8,128)(2,1)S(1)}, bf16[1,136,768]{2,1,0:T(8,128)(2,1)S(1)}, u32[]{:S(2)}, u32[]{:S(2)}) %collective-permute-start.2) | collective-permute-done | bytes 208928 | tf_op jit(solution)/shard_map/ppermute | solution.py:646
  36.8 3.2 %collective-permute-start.13 = (bf16[3,192,768]{2,1,0:T(8,128)(2,1)}, bf16[3,192,768]{2,1,0:T(8,128)(2,1)}, u32[]{:S(2)}, u32[]{:S(2)}) collective-permute-start(bf16[3,192,768]{2,1,0:T(8,128)(2,1)} %collective-permute-done.6.refs_13_), channel_id=1, source_target_pairs={{0,2},{2,0},{4,6},{6,4},{8,10},{10,8},{12,14},{14,12},{16,18},{18,... | collective-permute-start | bytes 2654216 | tf_op jit(solution)/shard_map/ppermute | solution.py:646
  47.3 10.2 %project.2 = (bf16[8,128,2304]{2,1,0:T(8,128)(2,1)}, s32[8,128,128]{2,1,0:T(8,128)S(1)}, bf16[3,768,768]{2,1,0:T(8,128)(2,1)}, bf16[128,768]{1,0:T(8,128)(2,1)S(1)}) custom-call(s32[6]{0:T(128)S(1)} %pad_add_fusion.spot_ref, bf16[1,136,768]{2,1,0:T(8,128)(2,1)S(1)} %maximum_bitcast_fusion.refs_0_, bf16[1,136,768]{2,1,0:T(8,128)(2,1)S(1)} %collective-permute-done.refs_1_, ...), custom_call_target="tpu_custom_call" | custom-call | flops 4480000000 | bytes 14000000 | tf_op jit(solution)/shard_map/project/pallas_call | solution.py:146
  58.0 9.7 %attend.2 = (f32[6,1,256]{2,1,0:T(1,128)S(1)}, f32[6,1,256]{2,1,0:T(1,128)S(1)}, f32[6,128,256]{2,1,0:T(8,128)S(1)}, f32[6,1,1,256]{3,2,1,0:T(1,128)S(1)}, bf16[12,1024,128]{2,1,0:T(8,128)(2,1)}) custom-call(bf16[1024,2304]{1,0:T(8,128)(2,1)} %bitcast.210, bf16[1024,2304]{1,0:T(8,128)(2,1)} %bitcast.211, bf16[1024,2304]{1,0:T(8,128)(2,1)} %bitcast.212, ...), custom_call_target="tpu_custom_call" | custom-call | flops 6553600000 | bytes 20480000 | tf_op jit(solution)/shard_map/attend/pallas_call | solution.py:464
  69.6 8.8 %project.3 = (bf16[8,128,2304]{2,1,0:T(8,128)(2,1)}, s32[8,128,128]{2,1,0:T(8,128)S(1)}) custom-call(s32[6]{0:T(128)S(1)} %pad_add_fusion.spot_ref, bf16[1,136,768]{2,1,0:T(8,128)(2,1)S(1)} %collective-permute-done.1.refs_0_, bf16[1,136,768]{2,1,0:T(8,128)(2,1)S(1)} %collective-permute-done.2.refs_1_, ...), custom_call_target="tpu_custom_call" | custom-call | flops 4480000000 | bytes 14000000 | tf_op jit(solution)/shard_map/project/pallas_call | solution.py:146
  78.4 10.3 %attend.3 = (f32[128,768]{1,0:T(8,128)S(1)}, f32[6,1,256]{2,1,0:T(1,128)S(1)}, f32[6,1,1,256]{3,2,1,0:T(1,128)S(1)}, bf16[12,1024,128]{2,1,0:T(8,128)(2,1)}) custom-call(bf16[1024,2304]{1,0:T(8,128)(2,1)} %bitcast.213, bf16[1024,2304]{1,0:T(8,128)(2,1)} %bitcast.216, bf16[1024,2304]{1,0:T(8,128)(2,1)} %bitcast.217, s32[1024,128]{1,0:T(8,128)S(1)} %bitcast.156, ...), custom_call_target="tpu_custom_call" | custom-call | flops 6553600000 | bytes 20480000 | tf_op jit(solution)/shard_map/attend/pallas_call | solution.py:464
  93.1 3.9 %collective-permute-done.21 = bf16[128,768]{1,0:T(8,128)(2,1)S(1)} collective-permute-done((bf16[128,768]{1,0:T(8,128)(2,1)S(1)}, bf16[128,768]{1,0:T(8,128)(2,1)S(1)}, u32[]{:S(2)}, u32[]{:S(2)}) %collective-permute-start.21) | collective-permute-done | bytes 196640 | tf_op jit(solution)/shard_map/ppermute | solution.py:650
  103.4 4.3 %collective-permute-done.22.got_ref = bf16[128,768]{1,0:T(8,128)(2,1)S(1)} collective-permute-done((bf16[128,768]{1,0:T(8,128)(2,1)S(1)}, bf16[128,768]{1,0:T(8,128)(2,1)S(1)}, u32[]{:S(2)}, u32[]{:S(2)}) %collective-permute-start.22) | collective-permute-done | bytes 196640 | tf_op jit(solution)/shard_map/ppermute | solution.py:650
  110.2 2.4 collective-permute-start.24
  121.5 10.0 %collective-permute-done.25 = bf16[1,128,896]{2,1,0:T(8,128)(2,1)} collective-permute-done((bf16[1,128,896]{2,1,0:T(8,128)(2,1)S(1)}, bf16[1,128,896]{2,1,0:T(8,128)(2,1)}, u32[]{:S(2)}, u32[]{:S(2)}) %collective-permute-start.25) | collective-permute-done | bytes 229408 | tf_op jit(solution)/shard_map/ppermute | solution.py:646
  133.1 3.2 %collective-permute-start.33 = (bf16[1,128,896]{2,1,0:T(8,128)(2,1)S(1)}, bf16[1,128,896]{2,1,0:T(8,128)(2,1)S(1)}, u32[]{:S(2)}, u32[]{:S(2)}) collective-permute-start(bf16[1,128,896]{2,1,0:T(8,128)(2,1)S(1)} %collective-permute-done.23), channel_id=1, source_target_pairs={{0,2},{2,0},{4,6},{6,4},{8,10},{10,8},{12,14},{14,12},{16,18},{18,... | collective-permute-start | bytes 688136 | tf_op jit(solution)/shard_map/ppermute | solution.py:646
  138.2 3.1 %collective-permute-start.32 = (bf16[1,128,896]{2,1,0:T(8,128)(2,1)S(1)}, bf16[1,128,896]{2,1,0:T(8,128)(2,1)S(1)}, u32[]{:S(2)}, u32[]{:S(2)}) collective-permute-start(bf16[1,128,896]{2,1,0:T(8,128)(2,1)S(1)} %bitcast.153), channel_id=1, source_target_pairs={{0,2},{2,0},{4,6},{6,4},{8,10},{10,8},{12,14},{14,12},{16,18},{18,... | collective-permute-start | bytes 688136 | tf_op jit(solution)/shard_map/ppermute | solution.py:646
  143.5 9.2 %query_back.1 = (bf16[12,1024,128]{2,1,0:T(8,128)(2,1)S(1)}, bf16[12,1024,128]{2,1,0:T(8,128)(2,1)}, bf16[128,768]{1,0:T(8,128)(2,1)S(1)}) custom-call(bf16[12,1024,128]{2,1,0:T(8,128)(2,1)S(1)} %copy-done.13, bf16[1024,2304]{1,0:T(8,128)(2,1)} %bitcast.214, bf16[1024,2304]{1,0:T(8,128)(2,1)} %bitcast.215, ...), custom_call_target="tpu_custom_call", output_to_operand_aliasing={{0}: (0, {}), {1}: (4, {})} | custom-call | flops 8192000000 | bytes 25600000 | tf_op jit(solution)/shard_map/query_back/pallas_call | solution.py:535
  154.2 5.6 %fusion.22 = f32[12,32]{1,0:T(8,128)S(1)} fusion(s32[1024,128]{1,0:T(8,128)S(1)} %bitcast.157, bf16[12,1024,128]{2,1,0:T(8,128)(2,1)} %get-tuple-element.164), kind=kOutput, calls=%fused_computation.42 | convolution fusion | flops 104857600 | bytes 3671552 | tf_op jit(solution)/shard_map/hkq,kqb->hb/dot_general | solution.py:887
  159.8 3.8 %fusion.28 = f32[12,32]{1,0:T(8,128)S(1)} fusion(f32[12,32]{1,0:T(8,128)S(1)} %fusion.22, s32[1024,128]{1,0:T(8,128)S(1)} %bitcast.155, bf16[12,1024,128]{2,1,0:T(8,128)(2,1)S(1)} %get-tuple-element.163), kind=kOutput, calls=%fused_computation.44 | convolution fusion | flops 104857984 | bytes 3673088 | tf_op jit(solution)/shard_map/hkq,kqb->hb/dot_general | solution.py:887
  167.5 15.9 %key_back.1 = bf16[2,128,768]{2,1,0:T(8,128)(2,1)} custom-call(bf16[128,896]{1,0:T(8,128)(2,1)} %copy-done.7, bf16[128,896]{1,0:T(8,128)(2,1)} %bitcast.182, bf16[128,896]{1,0:T(8,128)(2,1)} %bitcast.186, bf16[128,896]{1,0:T(8,128)(2,1)} %bitcast.188, bf16[128,896]{1,0:T(8,128)(2,1)} %bitcast.198, bf16[128,896]{1,0:T(8,128)(2,1)} %bitcast.190, ...), custom_call_target="tpu_custom_call" | custom-call | flops 12000000000 | bytes 37500000 | tf_op jit(solution)/shard_map/key_back/pallas_call | solution.py:606
  188.4 2.7 fusion.40
  192.5 2.5 fusion.82
  198.7 2.7 collective-permute-done.40
  207.3 5.3 %reduce-scatter.2.cloned.1.call-done = bf16[216,768]{1,0:T(8,128)(2,1)} async-done(((bf16[3456,768]{1,0:T(8,128)(2,1)}), bf16[216,768]{1,0:T(8,128)(2,1)}) %reduce-scatter.2.cloned.1.call-update) | async-done | bytes 331792 | tf_op jit(solution)/shard_map/reduce_scatter | solution.py:895
  218.1 9.1 %collective-permute-done.45 = bf16[4,80,768]{2,1,0:T(8,128)(2,1)S(1)} collective-permute-done((bf16[4,80,768]{2,1,0:T(8,128)(2,1)S(1)}, bf16[4,80,768]{2,1,0:T(8,128)(2,1)S(1)}, u32[]{:S(2)}, u32[]{:S(2)}) %collective-permute-start.45) | collective-permute-done | bytes 491552 | tf_op jit(solution)/shard_map/ppermute | solution.py:646
  230.1 5.5 %collective-permute-done.46 = bf16[1,80,768]{2,1,0:T(8,128)(2,1)S(1)} collective-permute-done((bf16[1,80,768]{2,1,0:T(8,128)(2,1)S(1)}, bf16[1,80,768]{2,1,0:T(8,128)(2,1)S(1)}, u32[]{:S(2)}, u32[]{:S(2)}) %collective-permute-start.46) | collective-permute-done | bytes 122912 | tf_op jit(solution)/shard_map/ppermute | solution.py:646
  235.7 3.1 collective-permute-done.47
  238.8 12.2 %collective-permute-done.48 = bf16[1,80,768]{2,1,0:T(8,128)(2,1)S(1)} collective-permute-done((bf16[1,80,768]{2,1,0:T(8,128)(2,1)S(1)}, bf16[1,80,768]{2,1,0:T(8,128)(2,1)S(1)}, u32[]{:S(2)}, u32[]{:S(2)}) %collective-permute-start.48) | collective-permute-done | bytes 122912 | tf_op jit(solution)/shard_map/ppermute | solution.py:646
  256.6 17.5 %collective-permute-done.51 = bf16[1,80,768]{2,1,0:T(8,128)(2,1)S(1)} collective-permute-done((bf16[1,80,768]{2,1,0:T(8,128)(2,1)S(1)}, bf16[1,80,768]{2,1,0:T(8,128)(2,1)S(1)}, u32[]{:S(2)}, u32[]{:S(2)}) %collective-permute-start.51) | collective-permute-done | bytes 122912 | tf_op jit(solution)/shard_map/ppermute | solution.py:646
  274.7 8.6 %collective-permute-done.52 = bf16[4,80,768]{2,1,0:T(8,128)(2,1)S(1)} collective-permute-done((bf16[4,80,768]{2,1,0:T(8,128)(2,1)S(1)}, bf16[4,80,768]{2,1,0:T(8,128)(2,1)S(1)}, u32[]{:S(2)}, u32[]{:S(2)}) %collective-permute-start.52) | collective-permute-done | bytes 491552 | tf_op jit(solution)/shard_map/ppermute | solution.py:646
  283.5 4.6 %collective-permute-start.53 = (bf16[8,80,768]{2,1,0:T(8,128)(2,1)S(1)}, bf16[8,80,768]{2,1,0:T(8,128)(2,1)S(1)}, u32[]{:S(2)}, u32[]{:S(2)}) collective-permute-start(bf16[8,80,768]{2,1,0:T(8,128)(2,1)S(1)} %maximum_select_fusion.2.near_ref), channel_id=1, source_target_pairs={{0,2},{2,0},{4,6},{6,4},{8,10},{10,8},{12,14},{14,12},{16,18},{18,... | collective-permute-start | bytes 2949128 | tf_op jit(solution)/shard_map/ppermute | solution.py:646
  290.5 2.8 unpack.1
  294.7 7.5 %spread.1 = (f32[16,96,768]{2,1,0:T(8,128)}, f32[16,24,3072]{2,1,0:T(8,128)}, f32[16,24,768]{2,1,0:T(8,128)}) custom-call(s32[6]{0:T(128)S(1)} %pad_add_fusion.spot_ref, bf16[16,216,768]{2,1,0:T(8,128)(2,1)} %bitcast.181), custom_call_target="tpu_custom_call" | custom-call | flops 4800000000 | bytes 15000000 | tf_op jit(solution)/shard_map/spread/pallas_call | solution.py:350
  (327 shorter events, 87.6 us)
Async XLA Ops:
  7.2 205.4 %reduce-scatter.2.cloned.1.call-start = ((), (), s32[]{:S(2)}) async-start(), calls=%async_computation.1 | async-start | bytes 5640192 | tf_op jit(solution)/shard_map/reduce_scatter | solution.py:895
  11.4 25.4 %collective-permute-start.6 = (bf16[3,192,768]{2,1,0:T(8,128)(2,1)}, bf16[3,192,768]{2,1,0:T(8,128)(2,1)}, u32[]{:S(2)}, u32[]{:S(2)}) collective-permute-start(bf16[3,192,768]{2,1,0:T(8,128)(2,1)} %pad_maximum_fusion.4), channel_id=1, source_target_pairs={{0,1},{1,0},{2,3},{3,2},{4,5},{5,4},{6,7},{7,6},{8,9},{9,8},{10,11... | collective-permute-start | bytes 2654216 | tf_op jit(solution)/shard_map/ppermute | solution.py:650
  11.8 11.2 %collective-permute-start.1 = (bf16[1,136,768]{2,1,0:T(8,128)(2,1)S(1)}, bf16[1,136,768]{2,1,0:T(8,128)(2,1)S(1)}, u32[]{:S(2)}, u32[]{:S(2)}) collective-permute-start(bf16[1,136,768]{2,1,0:T(8,128)(2,1)S(1)} %maximum_bitcast_fusion.refs_0_), channel_id=1, source_target_pairs={{0,16},{2,18},{4,20},{6,22},{8,24},{10,26},{12,28},{14,30},{16,0},... | collective-permute-start | bytes 626696 | tf_op jit(solution)/shard_map/ppermute | solution.py:646
  14.3 17.8 %collective-permute-start.2 = (bf16[1,136,768]{2,1,0:T(8,128)(2,1)S(1)}, bf16[1,136,768]{2,1,0:T(8,128)(2,1)S(1)}, u32[]{:S(2)}, u32[]{:S(2)}) collective-permute-start(bf16[1,136,768]{2,1,0:T(8,128)(2,1)S(1)} %maximum_bitcast_fusion.refs_0_), channel_id=1, source_target_pairs={{0,24},{2,26},{4,28},{6,30},{8,16},{10,18},{12,20},{14,22},{16,8},... | collective-permute-start | bytes 626696 | tf_op jit(solution)/shard_map/ppermute | solution.py:646
  14.4 17.6 %collective-permute-start.3 = (bf16[1,136,768]{2,1,0:T(8,128)(2,1)S(1)}, bf16[1,136,768]{2,1,0:T(8,128)(2,1)}, u32[]{:S(2)}, u32[]{:S(2)}) collective-permute-start(bf16[1,136,768]{2,1,0:T(8,128)(2,1)S(1)} %maximum_bitcast_fusion.refs_0_), channel_id=1, source_target_pairs={{0,4},{2,6},{4,0},{6,2},{8,12},{10,14},{12,8},{14,10},{16,20},{18,... | collective-permute-start | bytes 626696 | tf_op jit(solution)/shard_map/ppermute | solution.py:646
  41.2 16.2 %collective-permute-start.4 = (bf16[1,136,768]{2,1,0:T(8,128)(2,1)S(1)}, bf16[1,136,768]{2,1,0:T(8,128)(2,1)S(1)}, u32[]{:S(2)}, u32[]{:S(2)}) collective-permute-start(bf16[1,136,768]{2,1,0:T(8,128)(2,1)S(1)} %collective-permute-done.1.refs_0_), channel_id=1, source_target_pairs={{0,4},{2,6},{4,0},{6,2},{8,12},{10,14},{12,8},{14,10},{16,20},{18,... | collective-permute-start | bytes 626696 | tf_op jit(solution)/shard_map/ppermute | solution.py:646
  44.4 23.4 %collective-permute-start.14 = (bf16[1,136,768]{2,1,0:T(8,128)(2,1)S(1)}, bf16[1,136,768]{2,1,0:T(8,128)(2,1)S(1)}, u32[]{:S(2)}, u32[]{:S(2)}) collective-permute-start(bf16[1,136,768]{2,1,0:T(8,128)(2,1)S(1)} %collective-permute-done.1.refs_0_), channel_id=1, source_target_pairs={{0,2},{2,0},{4,6},{6,4},{8,10},{10,8},{12,14},{14,12},{16,18},{18,... | collective-permute-start | bytes 626696 | tf_op jit(solution)/shard_map/ppermute | solution.py:646
  44.5 12.9 %collective-permute-start.5 = (bf16[1,136,768]{2,1,0:T(8,128)(2,1)S(1)}, bf16[1,136,768]{2,1,0:T(8,128)(2,1)S(1)}, u32[]{:S(2)}, u32[]{:S(2)}) collective-permute-start(bf16[1,136,768]{2,1,0:T(8,128)(2,1)S(1)} %collective-permute-done.2.refs_1_), channel_id=1, source_target_pairs={{0,4},{2,6},{4,0},{6,2},{8,12},{10,14},{12,8},{14,10},{16,20},{18,... | collective-permute-start | bytes 626696 | tf_op jit(solution)/shard_map/ppermute | solution.py:646
  45.4 23.5 %collective-permute-start.15 = (bf16[1,136,768]{2,1,0:T(8,128)(2,1)S(1)}, bf16[1,136,768]{2,1,0:T(8,128)(2,1)S(1)}, u32[]{:S(2)}, u32[]{:S(2)}) collective-permute-start(bf16[1,136,768]{2,1,0:T(8,128)(2,1)S(1)} %collective-permute-done.2.refs_1_), channel_id=1, source_target_pairs={{0,2},{2,0},{4,6},{6,4},{8,10},{10,8},{12,14},{14,12},{16,18},{18,... | collective-permute-start | bytes 626696 | tf_op jit(solution)/shard_map/ppermute | solution.py:646
  46.0 22.8 %collective-permute-start.18 = (bf16[3,192,768]{2,1,0:T(8,128)(2,1)S(1)}, bf16[3,192,768]{2,1,0:T(8,128)(2,1)S(1)}, u32[]{:S(2)}, u32[]{:S(2)}) collective-permute-start(bf16[3,192,768]{2,1,0:T(8,128)(2,1)S(1)} %pad_maximum_fusion.5), channel_id=1, source_target_pairs={{0,1},{1,0},{2,3},{3,2},{4,5},{5,4},{6,7},{7,6},{8,9},{9,8},{10,11... | collective-permute-start | bytes 2654216 | tf_op jit(solution)/shard_map/ppermute | solution.py:650
  57.4 11.4 %collective-permute-start.16 = (bf16[1,136,768]{2,1,0:T(8,128)(2,1)S(1)}, bf16[1,136,768]{2,1,0:T(8,128)(2,1)S(1)}, u32[]{:S(2)}, u32[]{:S(2)}) collective-permute-start(bf16[1,136,768]{2,1,0:T(8,128)(2,1)S(1)} %collective-permute-done.4.refs_2_), channel_id=1, source_target_pairs={{0,2},{2,0},{4,6},{6,4},{8,10},{10,8},{12,14},{14,12},{16,18},{18,... | collective-permute-start | bytes 626696 | tf_op jit(solution)/shard_map/ppermute | solution.py:646
  57.9 11.0 %collective-permute-start.17 = (bf16[1,136,768]{2,1,0:T(8,128)(2,1)S(1)}, bf16[1,136,768]{2,1,0:T(8,128)(2,1)S(1)}, u32[]{:S(2)}, u32[]{:S(2)}) collective-permute-start(bf16[1,136,768]{2,1,0:T(8,128)(2,1)S(1)} %collective-permute-done.5.refs_3_), channel_id=1, source_target_pairs={{0,2},{2,0},{4,6},{6,4},{8,10},{10,8},{12,14},{14,12},{16,18},{18,... | collective-permute-start | bytes 626696 | tf_op jit(solution)/shard_map/ppermute | solution.py:646
  68.6 30.3 %collective-permute-start.20 = (bf16[128,768]{1,0:T(8,128)(2,1)S(1)}, bf16[128,768]{1,0:T(8,128)(2,1)S(1)}, u32[]{:S(2)}, u32[]{:S(2)}) collective-permute-start(bf16[128,768]{1,0:T(8,128)(2,1)S(1)} %bitcast.141), channel_id=1, source_target_pairs={{0,1},{1,0},{2,3},{3,2},{4,5},{5,4},{6,7},{7,6},{8,9},{9,8},{10,11... | collective-permute-start | bytes 589832 | tf_op jit(solution)/shard_map/ppermute | solution.py:650
  68.9 19.9 %collective-permute-start.19 = (bf16[3,192,768]{2,1,0:T(8,128)(2,1)S(1)}, bf16[3,192,768]{2,1,0:T(8,128)(2,1)S(1)}, u32[]{:S(2)}, u32[]{:S(2)}) collective-permute-start(bf16[3,192,768]{2,1,0:T(8,128)(2,1)S(1)} %collective-permute-done.18.got_ref), channel_id=1, source_target_pairs={{0,2},{2,0},{4,6},{6,4},{8,10},{10,8},{12,14},{14,12},{16,18},{18,... | collective-permute-start | bytes 2654216 | tf_op jit(solution)/shard_map/ppermute | solution.py:646
  110.1 9.9 %collective-permute-start.23 = (bf16[1,128,896]{2,1,0:T(8,128)(2,1)S(1)}, bf16[1,128,896]{2,1,0:T(8,128)(2,1)S(1)}, u32[]{:S(2)}, u32[]{:S(2)}) collective-permute-start(bf16[1,128,896]{2,1,0:T(8,128)(2,1)S(1)} %bitcast.149), channel_id=1, source_target_pairs={{0,8},{2,10},{4,12},{6,14},{8,0},{10,2},{12,4},{14,6},{16,24},{18,... | collective-permute-start | bytes 688136 | tf_op jit(solution)/shard_map/ppermute | solution.py:646
  110.2 11.3 %collective-permute-start.24 = (bf16[1,128,896]{2,1,0:T(8,128)(2,1)S(1)}, bf16[1,128,896]{2,1,0:T(8,128)(2,1)S(1)}, u32[]{:S(2)}, u32[]{:S(2)}) collective-permute-start(bf16[1,128,896]{2,1,0:T(8,128)(2,1)S(1)} %bitcast.150), channel_id=1, source_target_pairs={{0,16},{2,18},{4,20},{6,22},{8,24},{10,26},{12,28},{14,30},{16,0},... | collective-permute-start | bytes 688136 | tf_op jit(solution)/shard_map/ppermute | solution.py:646
  112.7 18.8 %collective-permute-start.25 = (bf16[1,128,896]{2,1,0:T(8,128)(2,1)S(1)}, bf16[1,128,896]{2,1,0:T(8,128)(2,1)}, u32[]{:S(2)}, u32[]{:S(2)}) collective-permute-start(bf16[1,128,896]{2,1,0:T(8,128)(2,1)S(1)} %bitcast.151), channel_id=1, source_target_pairs={{0,24},{2,26},{4,28},{6,30},{8,16},{10,18},{12,20},{14,22},{16,8},... | collective-permute-start | bytes 688136 | tf_op jit(solution)/shard_map/ppermute | solution.py:646
  112.9 18.6 %collective-permute-start.26 = (bf16[1,128,896]{2,1,0:T(8,128)(2,1)S(1)}, bf16[1,128,896]{2,1,0:T(8,128)(2,1)S(1)}, u32[]{:S(2)}, u32[]{:S(2)}) collective-permute-start(bf16[1,128,896]{2,1,0:T(8,128)(2,1)S(1)} %bitcast.152), channel_id=1, source_target_pairs={{0,4},{2,6},{4,0},{6,2},{8,12},{10,14},{12,8},{14,10},{16,20},{18,... | collective-permute-start | bytes 688136 | tf_op jit(solution)/shard_map/ppermute | solution.py:646
  132.3 162.4 %all-gather.2.cloned.1.call-start = ((), (), s32[]{:S(2)}) async-start(), calls=%async_computation.2 | async-start | bytes 5640192 | tf_op jit(solution)/shard_map/all_gather | solution.py:952
  133.1 30.9 %collective-permute-start.33 = (bf16[1,128,896]{2,1,0:T(8,128)(2,1)S(1)}, bf16[1,128,896]{2,1,0:T(8,128)(2,1)S(1)}, u32[]{:S(2)}, u32[]{:S(2)}) collective-permute-start(bf16[1,128,896]{2,1,0:T(8,128)(2,1)S(1)} %collective-permute-done.23), channel_id=1, source_target_pairs={{0,2},{2,0},{4,6},{6,4},{8,10},{10,8},{12,14},{14,12},{16,18},{18,... | collective-permute-start | bytes 688136 | tf_op jit(solution)/shard_map/ppermute | solution.py:646
  136.3 16.3 %collective-permute-start.29 = (bf16[1,128,896]{2,1,0:T(8,128)(2,1)S(1)}, bf16[1,128,896]{2,1,0:T(8,128)(2,1)S(1)}, u32[]{:S(2)}, u32[]{:S(2)}) collective-permute-start(bf16[1,128,896]{2,1,0:T(8,128)(2,1)S(1)} %collective-permute-done.24), channel_id=1, source_target_pairs={{0,4},{2,6},{4,0},{6,2},{8,12},{10,14},{12,8},{14,10},{16,20},{18,... | collective-permute-start | bytes 688136 | tf_op jit(solution)/shard_map/ppermute | solution.py:646
  137.1 29.0 %collective-permute-start.36 = (bf16[1,128,896]{2,1,0:T(8,128)(2,1)S(1)}, bf16[1,128,896]{2,1,0:T(8,128)(2,1)S(1)}, u32[]{:S(2)}, u32[]{:S(2)}) collective-permute-start(bf16[1,128,896]{2,1,0:T(8,128)(2,1)S(1)} %collective-permute-done.24), channel_id=1, source_target_pairs={{0,2},{2,0},{4,6},{6,4},{8,10},{10,8},{12,14},{14,12},{16,18},{18,... | collective-permute-start | bytes 688136 | tf_op jit(solution)/shard_map/ppermute | solution.py:646
  137.4 16.4 %collective-permute-start.30 = (bf16[1,128,896]{2,1,0:T(8,128)(2,1)}, bf16[1,128,896]{2,1,0:T(8,128)(2,1)S(1)}, u32[]{:S(2)}, u32[]{:S(2)}) collective-permute-start(bf16[1,128,896]{2,1,0:T(8,128)(2,1)} %collective-permute-done.25), channel_id=1, source_target_pairs={{0,4},{2,6},{4,0},{6,2},{8,12},{10,14},{12,8},{14,10},{16,20},{18,... | collective-permute-start | bytes 688136 | tf_op jit(solution)/shard_map/ppermute | solution.py:646
  138.2 25.5 %collective-permute-start.32 = (bf16[1,128,896]{2,1,0:T(8,128)(2,1)S(1)}, bf16[1,128,896]{2,1,0:T(8,128)(2,1)S(1)}, u32[]{:S(2)}, u32[]{:S(2)}) collective-permute-start(bf16[1,128,896]{2,1,0:T(8,128)(2,1)S(1)} %bitcast.153), channel_id=1, source_target_pairs={{0,2},{2,0},{4,6},{6,4},{8,10},{10,8},{12,14},{14,12},{16,18},{18,... | collective-permute-start | bytes 688136 | tf_op jit(solution)/shard_map/ppermute | solution.py:646
  152.7 11.6 %collective-permute-start.42 = (bf16[128,768]{1,0:T(8,128)(2,1)S(1)}, bf16[128,768]{1,0:T(8,128)(2,1)S(1)}, u32[]{:S(2)}, u32[]{:S(2)}) collective-permute-start(bf16[128,768]{1,0:T(8,128)(2,1)S(1)} %get-tuple-element.174), channel_id=1, source_target_pairs={{0,1},{1,0},{2,3},{3,2},{4,5},{5,4},{6,7},{7,6},{8,9},{9,8},{10,11... | collective-permute-start | bytes 589832 | tf_op jit(solution)/shard_map/ppermute | solution.py:650
  153.8 10.8 %collective-permute-start.31 = (bf16[1,128,896]{2,1,0:T(8,128)(2,1)S(1)}, bf16[1,128,896]{2,1,0:T(8,128)(2,1)S(1)}, u32[]{:S(2)}, u32[]{:S(2)}) collective-permute-start(bf16[1,128,896]{2,1,0:T(8,128)(2,1)S(1)} %collective-permute-done.30), channel_id=1, source_target_pairs={{0,2},{2,0},{4,6},{6,4},{8,10},{10,8},{12,14},{14,12},{16,18},{18,... | collective-permute-start | bytes 688136 | tf_op jit(solution)/shard_map/ppermute | solution.py:646
  165.7 31.5 %collective-permute-start.41 = (bf16[128,384]{1,0:T(8,128)(2,1)}, bf16[128,384]{1,0:T(8,128)(2,1)}, u32[]{:S(2)}, u32[]{:S(2)}) collective-permute-start(bf16[128,384]{1,0:T(8,128)(2,1)} %get-tuple-element.214), channel_id=1, source_target_pairs={{0,1},{1,0},{2,3},{3,2},{4,5},{5,4},{6,7},{7,6},{8,9},{9,8},{10,11... | collective-permute-start | bytes 294920 | tf_op jit(solution)/shard_map/ppermute | solution.py:650
  183.4 17.9 %collective-permute-start.39 = (bf16[2,128,768]{2,1,0:T(8,128)(2,1)}, bf16[2,128,768]{2,1,0:T(8,128)(2,1)S(1)}, u32[]{:S(2)}, u32[]{:S(2)}) collective-permute-start(bf16[2,128,768]{2,1,0:T(8,128)(2,1)} %key_back.1), channel_id=1, source_target_pairs={{0,1},{1,0},{2,3},{3,2},{4,5},{5,4},{6,7},{7,6},{8,9},{9,8},{10,11... | collective-permute-start | bytes 1179656 | tf_op jit(solution)/shard_map/ppermute | solution.py:650
  217.5 9.8 %collective-permute-start.45 = (bf16[4,80,768]{2,1,0:T(8,128)(2,1)S(1)}, bf16[4,80,768]{2,1,0:T(8,128)(2,1)S(1)}, u32[]{:S(2)}, u32[]{:S(2)}) collective-permute-start(bf16[4,80,768]{2,1,0:T(8,128)(2,1)S(1)} %constant_dynamic-slice_fusion.4), channel_id=1, source_target_pairs={{0,4},{2,6},{4,0},{6,2},{8,12},{10,14},{12,8},{14,10},{16,20},{18,... | collective-permute-start | bytes 1474568 | tf_op jit(solution)/shard_map/ppermute | solution.py:646
  228.4 10.3 %collective-permute-start.47 = (bf16[1,80,768]{2,1,0:T(8,128)(2,1)S(1)}, bf16[1,80,768]{2,1,0:T(8,128)(2,1)S(1)}, u32[]{:S(2)}, u32[]{:S(2)}) collective-permute-start(bf16[1,80,768]{2,1,0:T(8,128)(2,1)S(1)} %get-tuple-element.207), channel_id=1, source_target_pairs={{0,16},{2,18},{4,20},{6,22},{8,24},{10,26},{12,28},{14,30},{16,0},... | collective-permute-start | bytes 368648 | tf_op jit(solution)/shard_map/ppermute | solution.py:646
  229.8 21.1 %collective-permute-start.48 = (bf16[1,80,768]{2,1,0:T(8,128)(2,1)S(1)}, bf16[1,80,768]{2,1,0:T(8,128)(2,1)S(1)}, u32[]{:S(2)}, u32[]{:S(2)}) collective-permute-start(bf16[1,80,768]{2,1,0:T(8,128)(2,1)S(1)} %get-tuple-element.206), channel_id=1, source_target_pairs={{0,24},{2,26},{4,28},{6,30},{8,16},{10,18},{12,20},{14,22},{16,8},... | collective-permute-start | bytes 368648 | tf_op jit(solution)/shard_map/ppermute | solution.py:646
  252.4 21.7 %collective-permute-start.51 = (bf16[1,80,768]{2,1,0:T(8,128)(2,1)S(1)}, bf16[1,80,768]{2,1,0:T(8,128)(2,1)S(1)}, u32[]{:S(2)}, u32[]{:S(2)}) collective-permute-start(bf16[1,80,768]{2,1,0:T(8,128)(2,1)S(1)} %add_convert_fusion.2), channel_id=1, source_target_pairs={{0,24},{2,26},{4,28},{6,30},{8,16},{10,18},{12,20},{14,22},{16,8},... | collective-permute-start | bytes 368648 | tf_op jit(solution)/shard_map/ppermute | solution.py:646
  (82 other events, 665.4 us)
Sparse Core Ops, SparseCore 0:
  132.4 80.1 reduce-scatter.1
  217.6 73.4 all-gather.1

commit v2 on v1

--- a/solution.py
+++ b/solution.py
@@ -12,6 +12,7 @@
 NEG = -1000000000.0
 THRESHOLDS = (1, 2, 3, 4, 5, 6, 7, 8, 12, 16, 23, 32, 46, 64, 91)
 VMEM_BYTES = 50 * 1024 * 1024
+VMEM_LAST = 32 * 1024 * 1024
 VMEM_MOST = 63 * 1024 * 1024
 
 
@@ -364,7 +365,7 @@
             jax.ShapeDtypeStruct((size, tall, 4 * width), jnp.float32),
             jax.ShapeDtypeStruct((size, tall, width), jnp.float32),
         ],
-        compiler_params=pltpu.CompilerParams(vmem_limit_bytes=VMEM_BYTES),
+        compiler_params=pltpu.CompilerParams(vmem_limit_bytes=VMEM_LAST),
         cost_estimate=cost_of(6),
         name="spread",
     )(spot, full)

time: 310 us -> 309 us (level)
    unnamed x128 -> x130, local copies, waits for them, and re-layouts: 8.99 us -> 11.4 us
where the time goes in v2:
time: 309 us; the launch traced here: 308 us
  waiting for transfers between devices  106 us (34%)
  Pallas kernels  74.4 us (24%)
  starting transfers between devices  54.4 us (18%)
  matrix products  27.9 us (9%)
  local copies, waits for them, and re-layouts  23.1 us (7%)
  between operations  15.1 us (5%)
  other arithmetic  7.23 us (2%)
    ppermute x42, waiting for transfers between devices, swap_ctx(): return lax.ppermute(values, 'ctx', [(i, i ^ distance) for i in range(size)])  87.1 us
    ppermute x42, starting transfers between devices, swap_ctx(): return lax.ppermute(values, 'ctx', [(i, i ^ distance) for i in range(size)])  43.1 us
    pallas_call x2, Pallas kernels, attend(): pl.pallas_call(functools.partial(attend_kernel, tile, first), grid=(pairs...  20 us
    pallas_call x2, Pallas kernels, project(): pl.pallas_call(functools.partial(project_kernel, count, total, seqs, firs...  18.9 us
    pallas_call x1, Pallas kernels, key_back(): pl.pallas_call(functools.partial(key_back_kernel, count), grid=(pairs, n_...  15.9 us
    ppermute x13, waiting for transfers between devices, swap_pair(): return lax.ppermute(values, 'fsdp', [(0, 1), (1, 0)])  13.4 us
    unnamed x130, local copies, waits for them, and re-layouts  11.4 us
    ppermute x13, starting transfers between devices, swap_pair(): return lax.ppermute(values, 'fsdp', [(0, 1), (1, 0)])  11.3 us
  transfers between devices with their start and end apart: 57, of which 22 were waited for; matrix products, arithmetic and copies ran while one was open for 13% of the time, Pallas kernels for 22%

profile of v2, /device:TPU:11, one launch (start us, length us, event | category | flops | bytes accessed | tf_op | source)
XLA Modules:
  0.0 308.1 jit_solution(4639293755685954950)
XLA Ops:
  11.8 2.5 collective-permute-start.1
  15.8 2.7 collective-permute-done.refs_1_
  18.4 4.6 %collective-permute-done.1.refs_0_ = bf16[1,136,768]{2,1,0:T(8,128)(2,1)S(1)} collective-permute-done((bf16[1,136,768]{2,1,0:T(8,128)(2,1)S(1)}, bf16[1,136,768]{2,1,0:T(8,128)(2,1)S(1)}, u32[]{:S(2)}, u32[]{:S(2)}) %collective-permute-start.1) | collective-permute-done | bytes 208928 | tf_op jit(solution)/shard_map/ppermute | solution.py:647
  23.0 9.0 %collective-permute-done.2.refs_1_ = bf16[1,136,768]{2,1,0:T(8,128)(2,1)S(1)} collective-permute-done((bf16[1,136,768]{2,1,0:T(8,128)(2,1)S(1)}, bf16[1,136,768]{2,1,0:T(8,128)(2,1)S(1)}, u32[]{:S(2)}, u32[]{:S(2)}) %collective-permute-start.2) | collective-permute-done | bytes 208928 | tf_op jit(solution)/shard_map/ppermute | solution.py:647
  36.8 3.2 %collective-permute-start.13 = (bf16[3,192,768]{2,1,0:T(8,128)(2,1)}, bf16[3,192,768]{2,1,0:T(8,128)(2,1)}, u32[]{:S(2)}, u32[]{:S(2)}) collective-permute-start(bf16[3,192,768]{2,1,0:T(8,128)(2,1)} %collective-permute-done.6.refs_13_), channel_id=1, source_target_pairs={{0,2},{2,0},{4,6},{6,4},{8,10},{10,8},{12,14},{14,12},{16,18},{18,... | collective-permute-start | bytes 2654216 | tf_op jit(solution)/shard_map/ppermute | solution.py:647
  47.3 10.2 %project.2 = (bf16[8,128,2304]{2,1,0:T(8,128)(2,1)}, s32[8,128,128]{2,1,0:T(8,128)S(1)}, bf16[3,768,768]{2,1,0:T(8,128)(2,1)}, bf16[128,768]{1,0:T(8,128)(2,1)S(1)}) custom-call(s32[6]{0:T(128)S(1)} %pad_add_fusion.spot_ref, bf16[1,136,768]{2,1,0:T(8,128)(2,1)S(1)} %maximum_bitcast_fusion.refs_0_, bf16[1,136,768]{2,1,0:T(8,128)(2,1)S(1)} %collective-permute-done.refs_1_, ...), custom_call_target="tpu_custom_call" | custom-call | flops 4480000000 | bytes 14000000 | tf_op jit(solution)/shard_map/project/pallas_call | solution.py:147
  58.0 9.7 %attend.2 = (f32[6,1,256]{2,1,0:T(1,128)S(1)}, f32[6,1,256]{2,1,0:T(1,128)S(1)}, f32[6,128,256]{2,1,0:T(8,128)S(1)}, f32[6,1,1,256]{3,2,1,0:T(1,128)S(1)}, bf16[12,1024,128]{2,1,0:T(8,128)(2,1)}) custom-call(bf16[1024,2304]{1,0:T(8,128)(2,1)} %bitcast.210, bf16[1024,2304]{1,0:T(8,128)(2,1)} %bitcast.211, bf16[1024,2304]{1,0:T(8,128)(2,1)} %bitcast.212, ...), custom_call_target="tpu_custom_call" | custom-call | flops 6553600000 | bytes 20480000 | tf_op jit(solution)/shard_map/attend/pallas_call | solution.py:465
  69.6 8.8 %project.3 = (bf16[8,128,2304]{2,1,0:T(8,128)(2,1)}, s32[8,128,128]{2,1,0:T(8,128)S(1)}) custom-call(s32[6]{0:T(128)S(1)} %pad_add_fusion.spot_ref, bf16[1,136,768]{2,1,0:T(8,128)(2,1)S(1)} %collective-permute-done.1.refs_0_, bf16[1,136,768]{2,1,0:T(8,128)(2,1)S(1)} %collective-permute-done.2.refs_1_, ...), custom_call_target="tpu_custom_call" | custom-call | flops 4480000000 | bytes 14000000 | tf_op jit(solution)/shard_map/project/pallas_call | solution.py:147
  78.4 10.3 %attend.3 = (f32[128,768]{1,0:T(8,128)S(1)}, f32[6,1,256]{2,1,0:T(1,128)S(1)}, f32[6,1,1,256]{3,2,1,0:T(1,128)S(1)}, bf16[12,1024,128]{2,1,0:T(8,128)(2,1)}) custom-call(bf16[1024,2304]{1,0:T(8,128)(2,1)} %bitcast.213, bf16[1024,2304]{1,0:T(8,128)(2,1)} %bitcast.216, bf16[1024,2304]{1,0:T(8,128)(2,1)} %bitcast.217, s32[1024,128]{1,0:T(8,128)S(1)} %bitcast.157, ...), custom_call_target="tpu_custom_call" | custom-call | flops 6553600000 | bytes 20480000 | tf_op jit(solution)/shard_map/attend/pallas_call | solution.py:465
  93.1 3.9 %collective-permute-done.21 = bf16[128,768]{1,0:T(8,128)(2,1)S(1)} collective-permute-done((bf16[128,768]{1,0:T(8,128)(2,1)S(1)}, bf16[128,768]{1,0:T(8,128)(2,1)S(1)}, u32[]{:S(2)}, u32[]{:S(2)}) %collective-permute-start.21) | collective-permute-done | bytes 196640 | tf_op jit(solution)/shard_map/ppermute | solution.py:651
  103.4 4.2 %collective-permute-done.22.got_ref = bf16[128,768]{1,0:T(8,128)(2,1)S(1)} collective-permute-done((bf16[128,768]{1,0:T(8,128)(2,1)S(1)}, bf16[128,768]{1,0:T(8,128)(2,1)S(1)}, u32[]{:S(2)}, u32[]{:S(2)}) %collective-permute-start.22) | collective-permute-done | bytes 196640 | tf_op jit(solution)/shard_map/ppermute | solution.py:651
  121.5 10.0 %collective-permute-done.25 = bf16[1,128,896]{2,1,0:T(8,128)(2,1)} collective-permute-done((bf16[1,128,896]{2,1,0:T(8,128)(2,1)S(1)}, bf16[1,128,896]{2,1,0:T(8,128)(2,1)}, u32[]{:S(2)}, u32[]{:S(2)}) %collective-permute-start.25) | collective-permute-done | bytes 229408 | tf_op jit(solution)/shard_map/ppermute | solution.py:647
  133.1 3.2 %collective-permute-start.33 = (bf16[1,128,896]{2,1,0:T(8,128)(2,1)S(1)}, bf16[1,128,896]{2,1,0:T(8,128)(2,1)S(1)}, u32[]{:S(2)}, u32[]{:S(2)}) collective-permute-start(bf16[1,128,896]{2,1,0:T(8,128)(2,1)S(1)} %collective-permute-done.23), channel_id=1, source_target_pairs={{0,2},{2,0},{4,6},{6,4},{8,10},{10,8},{12,14},{14,12},{16,18},{18,... | collective-permute-start | bytes 688136 | tf_op jit(solution)/shard_map/ppermute | solution.py:647
  138.2 3.1 %collective-permute-start.32 = (bf16[1,128,896]{2,1,0:T(8,128)(2,1)S(1)}, bf16[1,128,896]{2,1,0:T(8,128)(2,1)S(1)}, u32[]{:S(2)}, u32[]{:S(2)}) collective-permute-start(bf16[1,128,896]{2,1,0:T(8,128)(2,1)S(1)} %bitcast.154), channel_id=1, source_target_pairs={{0,2},{2,0},{4,6},{6,4},{8,10},{10,8},{12,14},{14,12},{16,18},{18,... | collective-permute-start | bytes 688136 | tf_op jit(solution)/shard_map/ppermute | solution.py:647
  143.4 9.2 %query_back.1 = (bf16[12,1024,128]{2,1,0:T(8,128)(2,1)S(1)}, bf16[12,1024,128]{2,1,0:T(8,128)(2,1)}, bf16[128,768]{1,0:T(8,128)(2,1)S(1)}) custom-call(bf16[12,1024,128]{2,1,0:T(8,128)(2,1)S(1)} %copy-done.14, bf16[1024,2304]{1,0:T(8,128)(2,1)} %bitcast.214, bf16[1024,2304]{1,0:T(8,128)(2,1)} %bitcast.215, ...), custom_call_target="tpu_custom_call", output_to_operand_aliasing={{0}: (0, {}), {1}: (4, {})} | custom-call | flops 8192000000 | bytes 25600000 | tf_op jit(solution)/shard_map/query_back/pallas_call | solution.py:536
  154.2 5.6 %fusion.22 = f32[12,32]{1,0:T(8,128)S(1)} fusion(s32[1024,128]{1,0:T(8,128)S(1)} %bitcast.158, bf16[12,1024,128]{2,1,0:T(8,128)(2,1)} %get-tuple-element.164), kind=kOutput, calls=%fused_computation.42 | convolution fusion | flops 104857600 | bytes 3671552 | tf_op jit(solution)/shard_map/hkq,kqb->hb/dot_general | solution.py:888
  159.9 3.8 %fusion.28 = f32[12,32]{1,0:T(8,128)S(1)} fusion(f32[12,32]{1,0:T(8,128)S(1)} %fusion.22, s32[1024,128]{1,0:T(8,128)S(1)} %bitcast.156, bf16[12,1024,128]{2,1,0:T(8,128)(2,1)S(1)} %get-tuple-element.163), kind=kOutput, calls=%fused_computation.44 | convolution fusion | flops 104857984 | bytes 3673088 | tf_op jit(solution)/shard_map/hkq,kqb->hb/dot_general | solution.py:888
  167.4 15.9 %key_back.1 = bf16[2,128,768]{2,1,0:T(8,128)(2,1)} custom-call(bf16[128,896]{1,0:T(8,128)(2,1)} %copy-done.8, bf16[128,896]{1,0:T(8,128)(2,1)} %bitcast.182, bf16[128,896]{1,0:T(8,128)(2,1)} %bitcast.186, bf16[128,896]{1,0:T(8,128)(2,1)} %bitcast.188, bf16[128,896]{1,0:T(8,128)(2,1)} %bitcast.198, bf16[128,896]{1,0:T(8,128)(2,1)} %bitcast.190, ...), custom_call_target="tpu_custom_call" | custom-call | flops 12000000000 | bytes 37500000 | tf_op jit(solution)/shard_map/key_back/pallas_call | solution.py:607
  188.4 2.7 fusion.40
  192.4 2.5 fusion.82
  198.8 2.4 collective-permute-done.40
  207.2 5.5 %reduce-scatter.2.cloned.1.call-done = bf16[216,768]{1,0:T(8,128)(2,1)} async-done(((bf16[3456,768]{1,0:T(8,128)(2,1)}), bf16[216,768]{1,0:T(8,128)(2,1)}) %reduce-scatter.2.cloned.1.call-update) | async-done | bytes 331792 | tf_op jit(solution)/shard_map/reduce_scatter | solution.py:896
  218.6 8.8 %collective-permute-done.45 = bf16[4,80,768]{2,1,0:T(8,128)(2,1)S(1)} collective-permute-done((bf16[4,80,768]{2,1,0:T(8,128)(2,1)S(1)}, bf16[4,80,768]{2,1,0:T(8,128)(2,1)S(1)}, u32[]{:S(2)}, u32[]{:S(2)}) %collective-permute-start.45) | collective-permute-done | bytes 491552 | tf_op jit(solution)/shard_map/ppermute | solution.py:647
  230.3 4.3 %collective-permute-done.46 = bf16[1,80,768]{2,1,0:T(8,128)(2,1)S(1)} collective-permute-done((bf16[1,80,768]{2,1,0:T(8,128)(2,1)S(1)}, bf16[1,80,768]{2,1,0:T(8,128)(2,1)S(1)}, u32[]{:S(2)}, u32[]{:S(2)}) %collective-permute-start.46) | collective-permute-done | bytes 122912 | tf_op jit(solution)/shard_map/ppermute | solution.py:647
  234.6 4.2 %collective-permute-done.47 = bf16[1,80,768]{2,1,0:T(8,128)(2,1)S(1)} collective-permute-done((bf16[1,80,768]{2,1,0:T(8,128)(2,1)S(1)}, bf16[1,80,768]{2,1,0:T(8,128)(2,1)S(1)}, u32[]{:S(2)}, u32[]{:S(2)}) %collective-permute-start.47) | collective-permute-done | bytes 122912 | tf_op jit(solution)/shard_map/ppermute | solution.py:647
  238.9 12.1 %collective-permute-done.48 = bf16[1,80,768]{2,1,0:T(8,128)(2,1)S(1)} collective-permute-done((bf16[1,80,768]{2,1,0:T(8,128)(2,1)S(1)}, bf16[1,80,768]{2,1,0:T(8,128)(2,1)S(1)}, u32[]{:S(2)}, u32[]{:S(2)}) %collective-permute-start.48) | collective-permute-done | bytes 122912 | tf_op jit(solution)/shard_map/ppermute | solution.py:647
  256.6 16.7 %collective-permute-done.51 = bf16[1,80,768]{2,1,0:T(8,128)(2,1)S(1)} collective-permute-done((bf16[1,80,768]{2,1,0:T(8,128)(2,1)S(1)}, bf16[1,80,768]{2,1,0:T(8,128)(2,1)S(1)}, u32[]{:S(2)}, u32[]{:S(2)}) %collective-permute-start.51) | collective-permute-done | bytes 122912 | tf_op jit(solution)/shard_map/ppermute | solution.py:647
  274.8 7.1 %collective-permute-done.52 = bf16[4,80,768]{2,1,0:T(8,128)(2,1)S(1)} collective-permute-done((bf16[4,80,768]{2,1,0:T(8,128)(2,1)S(1)}, bf16[4,80,768]{2,1,0:T(8,128)(2,1)S(1)}, u32[]{:S(2)}, u32[]{:S(2)}) %collective-permute-start.52) | collective-permute-done | bytes 491552 | tf_op jit(solution)/shard_map/ppermute | solution.py:647
  282.0 5.4 %collective-permute-start.53 = (bf16[8,80,768]{2,1,0:T(8,128)(2,1)S(1)}, bf16[8,80,768]{2,1,0:T(8,128)(2,1)S(1)}, u32[]{:S(2)}, u32[]{:S(2)}) collective-permute-start(bf16[8,80,768]{2,1,0:T(8,128)(2,1)S(1)} %maximum_select_fusion.2.near_ref), channel_id=1, source_target_pairs={{0,2},{2,0},{4,6},{6,4},{8,10},{10,8},{12,14},{14,12},{16,18},{18,... | collective-permute-start | bytes 2949128 | tf_op jit(solution)/shard_map/ppermute | solution.py:647
  290.0 2.8 unpack.1
  294.1 2.5 copy-done.7
  296.7 4.7 %spread.1 = (f32[16,96,768]{2,1,0:T(8,128)}, f32[16,24,3072]{2,1,0:T(8,128)}, f32[16,24,768]{2,1,0:T(8,128)}) custom-call(s32[6]{0:T(128)S(1)} %pad_add_fusion.spot_ref, bf16[16,216,768]{2,1,0:T(8,128)(2,1)S(1)} %bitcast.149), custom_call_target="tpu_custom_call" | custom-call | flops 4800000000 | bytes 15000000 | tf_op jit(solution)/shard_map/spread/pallas_call | solution.py:351
  (329 shorter events, 91.6 us)
Async XLA Ops:
  7.2 205.5 %reduce-scatter.2.cloned.1.call-start = ((), (), s32[]{:S(2)}) async-start(), calls=%async_computation.1 | async-start | bytes 5640192 | tf_op jit(solution)/shard_map/reduce_scatter | solution.py:896
  11.4 25.4 %collective-permute-start.6 = (bf16[3,192,768]{2,1,0:T(8,128)(2,1)}, bf16[3,192,768]{2,1,0:T(8,128)(2,1)}, u32[]{:S(2)}, u32[]{:S(2)}) collective-permute-start(bf16[3,192,768]{2,1,0:T(8,128)(2,1)} %pad_maximum_fusion.4), channel_id=1, source_target_pairs={{0,1},{1,0},{2,3},{3,2},{4,5},{5,4},{6,7},{7,6},{8,9},{9,8},{10,11... | collective-permute-start | bytes 2654216 | tf_op jit(solution)/shard_map/ppermute | solution.py:651
  11.8 11.2 %collective-permute-start.1 = (bf16[1,136,768]{2,1,0:T(8,128)(2,1)S(1)}, bf16[1,136,768]{2,1,0:T(8,128)(2,1)S(1)}, u32[]{:S(2)}, u32[]{:S(2)}) collective-permute-start(bf16[1,136,768]{2,1,0:T(8,128)(2,1)S(1)} %maximum_bitcast_fusion.refs_0_), channel_id=1, source_target_pairs={{0,16},{2,18},{4,20},{6,22},{8,24},{10,26},{12,28},{14,30},{16,0},... | collective-permute-start | bytes 626696 | tf_op jit(solution)/shard_map/ppermute | solution.py:647
  14.3 17.8 %collective-permute-start.2 = (bf16[1,136,768]{2,1,0:T(8,128)(2,1)S(1)}, bf16[1,136,768]{2,1,0:T(8,128)(2,1)S(1)}, u32[]{:S(2)}, u32[]{:S(2)}) collective-permute-start(bf16[1,136,768]{2,1,0:T(8,128)(2,1)S(1)} %maximum_bitcast_fusion.refs_0_), channel_id=1, source_target_pairs={{0,24},{2,26},{4,28},{6,30},{8,16},{10,18},{12,20},{14,22},{16,8},... | collective-permute-start | bytes 626696 | tf_op jit(solution)/shard_map/ppermute | solution.py:647
  14.4 17.6 %collective-permute-start.3 = (bf16[1,136,768]{2,1,0:T(8,128)(2,1)S(1)}, bf16[1,136,768]{2,1,0:T(8,128)(2,1)}, u32[]{:S(2)}, u32[]{:S(2)}) collective-permute-start(bf16[1,136,768]{2,1,0:T(8,128)(2,1)S(1)} %maximum_bitcast_fusion.refs_0_), channel_id=1, source_target_pairs={{0,4},{2,6},{4,0},{6,2},{8,12},{10,14},{12,8},{14,10},{16,20},{18,... | collective-permute-start | bytes 626696 | tf_op jit(solution)/shard_map/ppermute | solution.py:647
  41.2 16.2 %collective-permute-start.4 = (bf16[1,136,768]{2,1,0:T(8,128)(2,1)S(1)}, bf16[1,136,768]{2,1,0:T(8,128)(2,1)S(1)}, u32[]{:S(2)}, u32[]{:S(2)}) collective-permute-start(bf16[1,136,768]{2,1,0:T(8,128)(2,1)S(1)} %collective-permute-done.1.refs_0_), channel_id=1, source_target_pairs={{0,4},{2,6},{4,0},{6,2},{8,12},{10,14},{12,8},{14,10},{16,20},{18,... | collective-permute-start | bytes 626696 | tf_op jit(solution)/shard_map/ppermute | solution.py:647
  44.4 23.4 %collective-permute-start.14 = (bf16[1,136,768]{2,1,0:T(8,128)(2,1)S(1)}, bf16[1,136,768]{2,1,0:T(8,128)(2,1)S(1)}, u32[]{:S(2)}, u32[]{:S(2)}) collective-permute-start(bf16[1,136,768]{2,1,0:T(8,128)(2,1)S(1)} %collective-permute-done.1.refs_0_), channel_id=1, source_target_pairs={{0,2},{2,0},{4,6},{6,4},{8,10},{10,8},{12,14},{14,12},{16,18},{18,... | collective-permute-start | bytes 626696 | tf_op jit(solution)/shard_map/ppermute | solution.py:647
  44.5 12.9 %collective-permute-start.5 = (bf16[1,136,768]{2,1,0:T(8,128)(2,1)S(1)}, bf16[1,136,768]{2,1,0:T(8,128)(2,1)S(1)}, u32[]{:S(2)}, u32[]{:S(2)}) collective-permute-start(bf16[1,136,768]{2,1,0:T(8,128)(2,1)S(1)} %collective-permute-done.2.refs_1_), channel_id=1, source_target_pairs={{0,4},{2,6},{4,0},{6,2},{8,12},{10,14},{12,8},{14,10},{16,20},{18,... | collective-permute-start | bytes 626696 | tf_op jit(solution)/shard_map/ppermute | solution.py:647
  45.4 23.5 %collective-permute-start.15 = (bf16[1,136,768]{2,1,0:T(8,128)(2,1)S(1)}, bf16[1,136,768]{2,1,0:T(8,128)(2,1)S(1)}, u32[]{:S(2)}, u32[]{:S(2)}) collective-permute-start(bf16[1,136,768]{2,1,0:T(8,128)(2,1)S(1)} %collective-permute-done.2.refs_1_), channel_id=1, source_target_pairs={{0,2},{2,0},{4,6},{6,4},{8,10},{10,8},{12,14},{14,12},{16,18},{18,... | collective-permute-start | bytes 626696 | tf_op jit(solution)/shard_map/ppermute | solution.py:647
  46.0 22.8 %collective-permute-start.18 = (bf16[3,192,768]{2,1,0:T(8,128)(2,1)S(1)}, bf16[3,192,768]{2,1,0:T(8,128)(2,1)S(1)}, u32[]{:S(2)}, u32[]{:S(2)}) collective-permute-start(bf16[3,192,768]{2,1,0:T(8,128)(2,1)S(1)} %pad_maximum_fusion.5), channel_id=1, source_target_pairs={{0,1},{1,0},{2,3},{3,2},{4,5},{5,4},{6,7},{7,6},{8,9},{9,8},{10,11... | collective-permute-start | bytes 2654216 | tf_op jit(solution)/shard_map/ppermute | solution.py:651
  57.4 11.4 %collective-permute-start.16 = (bf16[1,136,768]{2,1,0:T(8,128)(2,1)S(1)}, bf16[1,136,768]{2,1,0:T(8,128)(2,1)S(1)}, u32[]{:S(2)}, u32[]{:S(2)}) collective-permute-start(bf16[1,136,768]{2,1,0:T(8,128)(2,1)S(1)} %collective-permute-done.4.refs_2_), channel_id=1, source_target_pairs={{0,2},{2,0},{4,6},{6,4},{8,10},{10,8},{12,14},{14,12},{16,18},{18,... | collective-permute-start | bytes 626696 | tf_op jit(solution)/shard_map/ppermute | solution.py:647
  57.8 11.0 %collective-permute-start.17 = (bf16[1,136,768]{2,1,0:T(8,128)(2,1)S(1)}, bf16[1,136,768]{2,1,0:T(8,128)(2,1)S(1)}, u32[]{:S(2)}, u32[]{:S(2)}) collective-permute-start(bf16[1,136,768]{2,1,0:T(8,128)(2,1)S(1)} %collective-permute-done.5.refs_3_), channel_id=1, source_target_pairs={{0,2},{2,0},{4,6},{6,4},{8,10},{10,8},{12,14},{14,12},{16,18},{18,... | collective-permute-start | bytes 626696 | tf_op jit(solution)/shard_map/ppermute | solution.py:647
  68.6 30.3 %collective-permute-start.20 = (bf16[128,768]{1,0:T(8,128)(2,1)S(1)}, bf16[128,768]{1,0:T(8,128)(2,1)S(1)}, u32[]{:S(2)}, u32[]{:S(2)}) collective-permute-start(bf16[128,768]{1,0:T(8,128)(2,1)S(1)} %bitcast.141), channel_id=1, source_target_pairs={{0,1},{1,0},{2,3},{3,2},{4,5},{5,4},{6,7},{7,6},{8,9},{9,8},{10,11... | collective-permute-start | bytes 589832 | tf_op jit(solution)/shard_map/ppermute | solution.py:651
  68.9 19.9 %collective-permute-start.19 = (bf16[3,192,768]{2,1,0:T(8,128)(2,1)S(1)}, bf16[3,192,768]{2,1,0:T(8,128)(2,1)S(1)}, u32[]{:S(2)}, u32[]{:S(2)}) collective-permute-start(bf16[3,192,768]{2,1,0:T(8,128)(2,1)S(1)} %collective-permute-done.18.got_ref), channel_id=1, source_target_pairs={{0,2},{2,0},{4,6},{6,4},{8,10},{10,8},{12,14},{14,12},{16,18},{18,... | collective-permute-start | bytes 2654216 | tf_op jit(solution)/shard_map/ppermute | solution.py:647
  110.1 9.9 %collective-permute-start.23 = (bf16[1,128,896]{2,1,0:T(8,128)(2,1)S(1)}, bf16[1,128,896]{2,1,0:T(8,128)(2,1)S(1)}, u32[]{:S(2)}, u32[]{:S(2)}) collective-permute-start(bf16[1,128,896]{2,1,0:T(8,128)(2,1)S(1)} %bitcast.150), channel_id=1, source_target_pairs={{0,8},{2,10},{4,12},{6,14},{8,0},{10,2},{12,4},{14,6},{16,24},{18,... | collective-permute-start | bytes 688136 | tf_op jit(solution)/shard_map/ppermute | solution.py:647
  110.2 11.3 %collective-permute-start.24 = (bf16[1,128,896]{2,1,0:T(8,128)(2,1)S(1)}, bf16[1,128,896]{2,1,0:T(8,128)(2,1)S(1)}, u32[]{:S(2)}, u32[]{:S(2)}) collective-permute-start(bf16[1,128,896]{2,1,0:T(8,128)(2,1)S(1)} %bitcast.151), channel_id=1, source_target_pairs={{0,16},{2,18},{4,20},{6,22},{8,24},{10,26},{12,28},{14,30},{16,0},... | collective-permute-start | bytes 688136 | tf_op jit(solution)/shard_map/ppermute | solution.py:647
  112.6 18.8 %collective-permute-start.25 = (bf16[1,128,896]{2,1,0:T(8,128)(2,1)S(1)}, bf16[1,128,896]{2,1,0:T(8,128)(2,1)}, u32[]{:S(2)}, u32[]{:S(2)}) collective-permute-start(bf16[1,128,896]{2,1,0:T(8,128)(2,1)S(1)} %bitcast.152), channel_id=1, source_target_pairs={{0,24},{2,26},{4,28},{6,30},{8,16},{10,18},{12,20},{14,22},{16,8},... | collective-permute-start | bytes 688136 | tf_op jit(solution)/shard_map/ppermute | solution.py:647
  112.8 18.6 %collective-permute-start.26 = (bf16[1,128,896]{2,1,0:T(8,128)(2,1)S(1)}, bf16[1,128,896]{2,1,0:T(8,128)(2,1)S(1)}, u32[]{:S(2)}, u32[]{:S(2)}) collective-permute-start(bf16[1,128,896]{2,1,0:T(8,128)(2,1)S(1)} %bitcast.153), channel_id=1, source_target_pairs={{0,4},{2,6},{4,0},{6,2},{8,12},{10,14},{12,8},{14,10},{16,20},{18,... | collective-permute-start | bytes 688136 | tf_op jit(solution)/shard_map/ppermute | solution.py:647
  132.3 161.8 %all-gather.2.cloned.1.call-start = ((), (), s32[]{:S(2)}) async-start(), calls=%async_computation.2 | async-start | bytes 5640192 | tf_op jit(solution)/shard_map/all_gather | solution.py:953
  133.1 30.9 %collective-permute-start.33 = (bf16[1,128,896]{2,1,0:T(8,128)(2,1)S(1)}, bf16[1,128,896]{2,1,0:T(8,128)(2,1)S(1)}, u32[]{:S(2)}, u32[]{:S(2)}) collective-permute-start(bf16[1,128,896]{2,1,0:T(8,128)(2,1)S(1)} %collective-permute-done.23), channel_id=1, source_target_pairs={{0,2},{2,0},{4,6},{6,4},{8,10},{10,8},{12,14},{14,12},{16,18},{18,... | collective-permute-start | bytes 688136 | tf_op jit(solution)/shard_map/ppermute | solution.py:647
  136.3 16.3 %collective-permute-start.29 = (bf16[1,128,896]{2,1,0:T(8,128)(2,1)S(1)}, bf16[1,128,896]{2,1,0:T(8,128)(2,1)S(1)}, u32[]{:S(2)}, u32[]{:S(2)}) collective-permute-start(bf16[1,128,896]{2,1,0:T(8,128)(2,1)S(1)} %collective-permute-done.24), channel_id=1, source_target_pairs={{0,4},{2,6},{4,0},{6,2},{8,12},{10,14},{12,8},{14,10},{16,20},{18,... | collective-permute-start | bytes 688136 | tf_op jit(solution)/shard_map/ppermute | solution.py:647
  137.1 28.9 %collective-permute-start.36 = (bf16[1,128,896]{2,1,0:T(8,128)(2,1)S(1)}, bf16[1,128,896]{2,1,0:T(8,128)(2,1)S(1)}, u32[]{:S(2)}, u32[]{:S(2)}) collective-permute-start(bf16[1,128,896]{2,1,0:T(8,128)(2,1)S(1)} %collective-permute-done.24), channel_id=1, source_target_pairs={{0,2},{2,0},{4,6},{6,4},{8,10},{10,8},{12,14},{14,12},{16,18},{18,... | collective-permute-start | bytes 688136 | tf_op jit(solution)/shard_map/ppermute | solution.py:647
  137.4 16.4 %collective-permute-start.30 = (bf16[1,128,896]{2,1,0:T(8,128)(2,1)}, bf16[1,128,896]{2,1,0:T(8,128)(2,1)S(1)}, u32[]{:S(2)}, u32[]{:S(2)}) collective-permute-start(bf16[1,128,896]{2,1,0:T(8,128)(2,1)} %collective-permute-done.25), channel_id=1, source_target_pairs={{0,4},{2,6},{4,0},{6,2},{8,12},{10,14},{12,8},{14,10},{16,20},{18,... | collective-permute-start | bytes 688136 | tf_op jit(solution)/shard_map/ppermute | solution.py:647
  138.2 25.6 %collective-permute-start.32 = (bf16[1,128,896]{2,1,0:T(8,128)(2,1)S(1)}, bf16[1,128,896]{2,1,0:T(8,128)(2,1)S(1)}, u32[]{:S(2)}, u32[]{:S(2)}) collective-permute-start(bf16[1,128,896]{2,1,0:T(8,128)(2,1)S(1)} %bitcast.154), channel_id=1, source_target_pairs={{0,2},{2,0},{4,6},{6,4},{8,10},{10,8},{12,14},{14,12},{16,18},{18,... | collective-permute-start | bytes 688136 | tf_op jit(solution)/shard_map/ppermute | solution.py:647
  152.6 11.8 %collective-permute-start.42 = (bf16[128,768]{1,0:T(8,128)(2,1)S(1)}, bf16[128,768]{1,0:T(8,128)(2,1)S(1)}, u32[]{:S(2)}, u32[]{:S(2)}) collective-permute-start(bf16[128,768]{1,0:T(8,128)(2,1)S(1)} %get-tuple-element.174), channel_id=1, source_target_pairs={{0,1},{1,0},{2,3},{3,2},{4,5},{5,4},{6,7},{7,6},{8,9},{9,8},{10,11... | collective-permute-start | bytes 589832 | tf_op jit(solution)/shard_map/ppermute | solution.py:651
  153.8 10.8 %collective-permute-start.31 = (bf16[1,128,896]{2,1,0:T(8,128)(2,1)S(1)}, bf16[1,128,896]{2,1,0:T(8,128)(2,1)S(1)}, u32[]{:S(2)}, u32[]{:S(2)}) collective-permute-start(bf16[1,128,896]{2,1,0:T(8,128)(2,1)S(1)} %collective-permute-done.30), channel_id=1, source_target_pairs={{0,2},{2,0},{4,6},{6,4},{8,10},{10,8},{12,14},{14,12},{16,18},{18,... | collective-permute-start | bytes 688136 | tf_op jit(solution)/shard_map/ppermute | solution.py:647
  165.8 31.5 %collective-permute-start.41 = (bf16[128,384]{1,0:T(8,128)(2,1)}, bf16[128,384]{1,0:T(8,128)(2,1)}, u32[]{:S(2)}, u32[]{:S(2)}) collective-permute-start(bf16[128,384]{1,0:T(8,128)(2,1)} %get-tuple-element.214), channel_id=1, source_target_pairs={{0,1},{1,0},{2,3},{3,2},{4,5},{5,4},{6,7},{7,6},{8,9},{9,8},{10,11... | collective-permute-start | bytes 294920 | tf_op jit(solution)/shard_map/ppermute | solution.py:651
  183.4 17.9 %collective-permute-start.39 = (bf16[2,128,768]{2,1,0:T(8,128)(2,1)}, bf16[2,128,768]{2,1,0:T(8,128)(2,1)S(1)}, u32[]{:S(2)}, u32[]{:S(2)}) collective-permute-start(bf16[2,128,768]{2,1,0:T(8,128)(2,1)} %key_back.1), channel_id=1, source_target_pairs={{0,1},{1,0},{2,3},{3,2},{4,5},{5,4},{6,7},{7,6},{8,9},{9,8},{10,11... | collective-permute-start | bytes 1179656 | tf_op jit(solution)/shard_map/ppermute | solution.py:651
  217.6 9.9 %collective-permute-start.45 = (bf16[4,80,768]{2,1,0:T(8,128)(2,1)S(1)}, bf16[4,80,768]{2,1,0:T(8,128)(2,1)S(1)}, u32[]{:S(2)}, u32[]{:S(2)}) collective-permute-start(bf16[4,80,768]{2,1,0:T(8,128)(2,1)S(1)} %constant_dynamic-slice_fusion.4), channel_id=1, source_target_pairs={{0,4},{2,6},{4,0},{6,2},{8,12},{10,14},{12,8},{14,10},{16,20},{18,... | collective-permute-start | bytes 1474568 | tf_op jit(solution)/shard_map/ppermute | solution.py:647
  228.2 10.6 %collective-permute-start.47 = (bf16[1,80,768]{2,1,0:T(8,128)(2,1)S(1)}, bf16[1,80,768]{2,1,0:T(8,128)(2,1)S(1)}, u32[]{:S(2)}, u32[]{:S(2)}) collective-permute-start(bf16[1,80,768]{2,1,0:T(8,128)(2,1)S(1)} %get-tuple-element.207), channel_id=1, source_target_pairs={{0,16},{2,18},{4,20},{6,22},{8,24},{10,26},{12,28},{14,30},{16,0},... | collective-permute-start | bytes 368648 | tf_op jit(solution)/shard_map/ppermute | solution.py:647
  230.0 21.0 %collective-permute-start.48 = (bf16[1,80,768]{2,1,0:T(8,128)(2,1)S(1)}, bf16[1,80,768]{2,1,0:T(8,128)(2,1)S(1)}, u32[]{:S(2)}, u32[]{:S(2)}) collective-permute-start(bf16[1,80,768]{2,1,0:T(8,128)(2,1)S(1)} %get-tuple-element.206), channel_id=1, source_target_pairs={{0,24},{2,26},{4,28},{6,30},{8,16},{10,18},{12,20},{14,22},{16,8},... | collective-permute-start | bytes 368648 | tf_op jit(solution)/shard_map/ppermute | solution.py:647
  252.5 20.9 %collective-permute-start.51 = (bf16[1,80,768]{2,1,0:T(8,128)(2,1)S(1)}, bf16[1,80,768]{2,1,0:T(8,128)(2,1)S(1)}, u32[]{:S(2)}, u32[]{:S(2)}) collective-permute-start(bf16[1,80,768]{2,1,0:T(8,128)(2,1)S(1)} %add_convert_fusion.2), channel_id=1, source_target_pairs={{0,24},{2,26},{4,28},{6,30},{8,16},{10,18},{12,20},{14,22},{16,8},... | collective-permute-start | bytes 368648 | tf_op jit(solution)/shard_map/ppermute | solution.py:647
  (83 other events, 665.2 us)
Sparse Core Ops, SparseCore 0:
  132.4 80.2 reduce-scatter.1
  217.7 72.8 all-gather.1
